TPU v7x, 128 devices: a whole 4x4x4 slice. The times are simulated.
128 devices in a mesh: sub: 128 (over x, z, y, core).
Axes of the slice: x: 4, y: 4, z: 4, core: 2. Of those that a mesh axis runs over, the one named last changes fastest.
Arguments:
- gap_loads: bfloat16 [256, 2048, 128], P('sub')
- flexibility: bfloat16 [256, 2048, 2048], P('sub'), as said below
- corner_coupling: bfloat16 [256, 16, 2048], P('sub'), may hold values from -0.5 to 0.5
- corner_ids: int32 [256, 16], P('sub'), may hold values from 0 to 1023
- coarse_inverse: float32 [1024, 1024], P('sub'), as said below
- adjacency: int32 [256, 4], P('sub'), may hold values from 0 to 255, as said below
Outputs:
- multipliers: float32 [256, 2048, 128], P('sub')
- residual: float32 [256, 2048, 128], P('sub')
Inputs may be any that keep to these rules, and one draw needn't show every extreme that they name: Subdomain s = d * 2 + i lies on device d. Its partner across face f lies on device d XOR 2^f, and the pairing is mutual: adjacency[adjacency[s, f], f] = s. Each flexibility[s] is symmetric positive definite. coarse_inverse is symmetric positive definite.
All inputs are finite; a program needn't handle non-finite values.
Results may differ from a plain program's by a relative error of at most 0.019.
Values may be sent and summed in bfloat16 or wider, within the bound.
A program may use at most 128 MiB of HBM per device.

v0:
```python
import jax
import jax.numpy as jnp
from jax import lax
from jax.sharding import PartitionSpec as P

ITERS = 3


def swapped(value, axis, distance):
    mask = 2**distance
    pairs = [(source, source ^ mask) for source in range(lax.axis_size(axis))]
    return lax.ppermute(value, axis, pairs)


def load_jump(gap_loads, adjacency):
    sub_count = gap_loads.shape[0]
    face_width = gap_loads.shape[1] // adjacency.shape[1]
    pieces = []
    for face_round in range(adjacency.shape[1]):
        face_block = gap_loads[:, face_round * face_width : (face_round + 1) * face_width, :]
        received = swapped(face_block, "sub", face_round)
        partner = jnp.take(received, adjacency[:, face_round] % sub_count, axis=0)
        pieces.append(face_block.astype(jnp.float32) - partner.astype(jnp.float32))
    return jnp.concatenate(pieces, axis=1)


def field_jump(total, adjacency):
    sub_count = total.shape[0]
    face_width = total.shape[1] // adjacency.shape[1]
    pieces = []
    for face_round in range(adjacency.shape[1]):
        face_block = total[:, face_round * face_width : (face_round + 1) * face_width, :]
        received = swapped(face_block.astype(jnp.bfloat16), "sub", face_round).astype(
            face_block.dtype
        )
        partner = jnp.take(received, adjacency[:, face_round] % sub_count, axis=0)
        pieces.append(face_block - partner)
    return jnp.concatenate(pieces, axis=1)


def apply_operator(direction, flexibility, corner_coupling, corner_ids, coarse_inverse, adjacency):
    rounded = direction.astype(jnp.bfloat16)
    local_part = jnp.einsum(
        "sij,sjr->sir", flexibility, rounded, preferred_element_type=jnp.float32
    )
    corner_terms = jnp.einsum(
        "skj,sjr->skr", corner_coupling, rounded, preferred_element_type=jnp.float32
    )
    loads_count = direction.shape[2]
    corner_terms = corner_terms.reshape(-1, loads_count)
    corner_list = corner_ids.reshape(-1)
    coarse_count = coarse_inverse.shape[1]
    indicator = (corner_list[:, None] == jnp.arange(coarse_count, dtype=jnp.int32)[None, :]).astype(
        jnp.float32
    )
    coarse_part = jnp.dot(indicator.T, corner_terms, precision=lax.Precision.HIGHEST)
    coarse_rhs = lax.psum(coarse_part, "sub")
    solved_rows = jnp.dot(coarse_inverse, coarse_rhs, precision=lax.Precision.HIGHEST)
    coarse_sol = lax.all_gather(solved_rows, "sub", axis=0, tiled=True)
    corner_values = jnp.dot(indicator, coarse_sol, precision=lax.Precision.HIGHEST)
    corner_values = corner_values.reshape(
        corner_coupling.shape[0], corner_coupling.shape[1], loads_count
    )
    total = local_part + jnp.einsum(
        "skn,skr->snr",
        corner_coupling.astype(jnp.float32),
        corner_values,
        precision=lax.Precision.HIGHEST,
    )
    return field_jump(total, adjacency)


def squares(residual):
    return lax.psum(jnp.sum(residual * residual, axis=(0, 1)), "sub")


def shards(gap_loads, flexibility, corner_coupling, corner_ids, coarse_inverse, adjacency):
    gap = load_jump(gap_loads, adjacency)
    multipliers = jnp.zeros_like(gap)
    residual = gap
    direction = gap
    norm_now = squares(residual)
    for iteration in range(ITERS):
        applied = apply_operator(
            direction, flexibility, corner_coupling, corner_ids, coarse_inverse, adjacency
        )
        curvature = lax.psum(jnp.sum(direction * applied, axis=(0, 1)), "sub")
        step_size = norm_now / curvature
        multipliers = multipliers + step_size * direction
        residual = residual - step_size * applied
        norm_next = squares(residual)
        direction = residual + norm_next / norm_now * direction
        norm_now = norm_next
    return (multipliers, residual)


def solution(mesh):
    return jax.shard_map(
        shards,
        mesh=mesh,
        in_specs=(
            P("sub", None, None),
            P("sub", None, None),
            P("sub", None, None),
            P("sub", None),
            P("sub", None),
            P("sub", None),
        ),
        out_specs=(P("sub", None, None), P("sub", None, None)),
        check_vma=False,
    )
```

profile of v0, /device:TPU:1, one launch (start us, length us, event | category | flops | bytes accessed | tf_op | source)
XLA Modules:
  0.0 1010.3 jit_solution(1199713559107756604)
XLA Ops:
  8.7 2.5 collective-permute-start.3
  12.9 2.7 collective-permute-start.2
  15.7 1.6 collective-permute-start
  19.3 7.0 collective-permute-done.2
  29.9 12.7 %fusion.13 = f32[2,128,2048]{2,1,0:T(8,128)} fusion(bf16[2,2048,2048]{2,1,0:T(8,128)(2,1)} %param.11, f32[2,512,128]{1,2,0:T(8,128)S(1)} %convert_subtract_fusion, f32[2,512,128]{1,2,0:T(8,128)S(1)} %convert_subtract_fusion.1, f32[2,512,128]{1,2,0:T(8,128)S(1)} %convert_subtract_fusion.2, f32[2,512,128]{1,2,0:T(8,128)S(1)} %convert_subtract_fusion.3), kind=kOutput, calls=%fused_computation.63 | convolution fusion | flops 2151677952 | bytes 20971520 | tf_op jit(solution)/shard_map/sij,sjr->sir/dot_general | solution.py:43
  42.6 133.2 %all-reduce.5.cloned.1.call-done = f32[1024,128]{1,0:T(8,128)} async-done(((f32[1024,128]{1,0:T(8,128)}), f32[1024,128]{1,0:T(8,128)}) %all-reduce.5.cloned.1.call-update) | async-done | bytes 524304 | tf_op jit(solution)/shard_map/psum | solution.py:57
  177.2 34.8 %all_gather.9 = f32[1024,128]{1,0:T(8,128)S(1)} all-gather(f32[8,128]{1,0:T(8,128)S(1)} %convolution_bitcast_fusion.2), channel_id=1, replica_groups=mesh['sub'=128] {'sub'}, dimensions={0}, use_global_device_ids=true | all-gather | bytes 528384 | tf_op jit(solution)/shard_map/all_gather | solution.py:59
  212.3 2.7 fusion.2
  221.0 4.2 collective-permute-done.7
  229.1 1.9 collective-permute-done.5
  232.4 2.7 select_subtract_fusion.11
  236.0 63.6 %all-reduce = (f32[128]{0:T(128)S(1)}, f32[128]{0:T(128)S(1)}) all-reduce(f32[128]{0:T(128)S(1)} %get-tuple-element.9, f32[128]{0:T(128)S(1)} %get-tuple-element.8), channel_id=1, replica_groups=mesh['sub'=128] {'sub'}, use_global_device_ids=true, to_apply=%region_1.3 | all-reduce | flops 256 | bytes 2048 | tf_op jit(solution)/shard_map/psum | solution.py:74
  299.7 1.6 multiply_reduce_fusion.3
  301.3 63.0 %psum.66 = f32[128]{0:T(128)S(1)} all-reduce(f32[128]{0:T(128)S(1)} %multiply_reduce_fusion.3), channel_id=1, replica_groups=mesh['sub'=128] {'sub'}, use_global_device_ids=true, to_apply=%region_6.9 | all-reduce | flops 128 | bytes 1024 | tf_op jit(solution)/shard_map/psum | solution.py:74
  364.3 2.4 multiply_add_fusion.2
  368.6 12.7 %fusion.9 = f32[2,128,2048]{2,1,0:T(8,128)} fusion(bf16[2,2048,2048]{2,1,0:T(8,128)(2,1)} %param.11, f32[2,2048,128]{1,2,0:T(8,128)S(1)} %multiply_add_fusion.2), kind=kOutput, calls=%fused_computation.59 | convolution fusion | flops 2148007936 | bytes 20971520 | tf_op jit(solution)/shard_map/sij,sjr->sir/dot_general | solution.py:43
  381.3 129.3 %all-reduce.7.cloned.1.call-done = f32[1024,128]{1,0:T(8,128)} async-done(((f32[1024,128]{1,0:T(8,128)}), f32[1024,128]{1,0:T(8,128)}) %all-reduce.7.cloned.1.call-update) | async-done | bytes 524304 | tf_op jit(solution)/shard_map/psum | solution.py:57
  512.1 34.8 %all_gather.10 = f32[1024,128]{1,0:T(8,128)S(1)} all-gather(f32[8,128]{1,0:T(8,128)S(1)} %convolution_bitcast_fusion.1), channel_id=1, replica_groups=mesh['sub'=128] {'sub'}, dimensions={0}, use_global_device_ids=true | all-gather | bytes 528384 | tf_op jit(solution)/shard_map/all_gather | solution.py:59
  547.2 2.7 fusion.1
  555.1 2.4 gather_fusion.8
  557.5 2.6 collective-permute-done.11
  560.1 1.8 convert_element_type.136
  561.9 2.4 gather_fusion.11
  564.3 1.8 convert_element_type.134
  566.1 2.4 gather_fusion.10
  568.5 1.8 convert_element_type.132
  570.3 2.4 gather_fusion.9
  572.8 2.8 select_subtract_fusion.7
  577.3 62.9 %psum.68 = f32[128]{0:T(128)S(1)} all-reduce(f32[128]{0:T(128)S(1)} %multiply_reduce_fusion.2), channel_id=1, replica_groups=mesh['sub'=128] {'sub'}, use_global_device_ids=true, to_apply=%region_9.12 | all-reduce | flops 128 | bytes 1024 | tf_op jit(solution)/shard_map/psum | solution.py:87
  640.3 3.7 multiply_reduce_fusion.1
  644.0 73.9 %psum.69 = f32[128]{0:T(128)S(1)} all-reduce(f32[128]{0:T(128)S(1)} %get-tuple-element.16), channel_id=1, replica_groups=mesh['sub'=128] {'sub'}, use_global_device_ids=true, to_apply=%region_11.14 | all-reduce | flops 128 | bytes 1024 | tf_op jit(solution)/shard_map/psum | solution.py:74
  717.9 2.0 multiply_add_fusion.1
  723.1 13.4 %fusion.5 = f32[2,128,2048]{2,1,0:T(8,128)} fusion(bf16[2,2048,2048]{2,1,0:T(8,128)(2,1)} %param.11, f32[2,2048,128]{1,2,0:T(8,128)} %copy-done.1), kind=kOutput, calls=%fused_computation.55 | convolution fusion | flops 2148007936 | bytes 20971520 | tf_op jit(solution)/shard_map/sij,sjr->sir/dot_general | solution.py:43
  736.5 128.3 %all-reduce.9.cloned.1.call-done = f32[1024,128]{1,0:T(8,128)} async-done(((f32[1024,128]{1,0:T(8,128)}), f32[1024,128]{1,0:T(8,128)}) %all-reduce.9.cloned.1.call-update) | async-done | bytes 524304 | tf_op jit(solution)/shard_map/psum | solution.py:57
  866.3 34.8 %all_gather.11 = f32[1024,128]{1,0:T(8,128)S(1)} all-gather(f32[8,128]{1,0:T(8,128)S(1)} %convolution_bitcast_fusion), channel_id=1, replica_groups=mesh['sub'=128] {'sub'}, dimensions={0}, use_global_device_ids=true | all-gather | bytes 528384 | tf_op jit(solution)/shard_map/all_gather | solution.py:59
  901.4 2.7 fusion
  909.3 2.4 gather_fusion.12
  911.7 2.6 collective-permute-done.15
  914.3 1.8 convert_element_type.145
  916.1 2.4 gather_fusion.15
  918.5 1.8 convert_element_type.143
  920.3 2.4 gather_fusion.14
  923.6 2.4 gather_fusion.13
  926.0 3.0 select_subtract_fusion.3
  930.8 62.9 %psum.71 = f32[128]{0:T(128)S(1)} all-reduce(f32[128]{0:T(128)S(1)} %multiply_reduce_fusion), channel_id=1, replica_groups=mesh['sub'=128] {'sub'}, use_global_device_ids=true, to_apply=%region_14.17 | all-reduce | flops 128 | bytes 1024 | tf_op jit(solution)/shard_map/psum | solution.py:87
  993.7 5.0 multiply_subtract_fusion
  998.8 3.0 copy.25
  1001.8 1.8 copy.24
  (159 shorter events, 46.0 us)
Async XLA Ops:
  7.2 20.7 %copy-start = (bf16[2,16,2048]{2,1,0:T(8,128)(2,1)S(1)}, bf16[2,16,2048]{2,1,0:T(8,128)(2,1)}, u32[]{:S(2)}) copy-start(bf16[2,16,2048]{2,1,0:T(8,128)(2,1)} %param.12) | copy-start | bytes 393220
  7.2 10.2 %copy-start.22 = (s32[2,4]{1,0:T(2,128)S(1)}, s32[2,4]{1,0:T(2,128)}, u32[]{:S(2)}) copy-start(s32[2,4]{1,0:T(2,128)} %param.15) | copy-start | bytes 100
  7.2 10.5 %copy-start.33 = (s32[2,16]{1,0:T(2,128)S(1)}, s32[2,16]{1,0:T(2,128)}, u32[]{:S(2)}) copy-start(s32[2,16]{1,0:T(2,128)} %param.13) | copy-start | bytes 388
  7.2 168.6 %all-reduce.5.cloned.1.call-start = ((), (), s32[]{:S(2)}) async-start(), calls=%async_computation | async-start | bytes 1048576 | tf_op jit(solution)/shard_map/psum | solution.py:57
  8.7 9.2 collective-permute-start.3
  11.4 7.2 collective-permute-start.1
  12.9 13.5 %collective-permute-start.2 = (bf16[2,512,128]{1,2,0:T(8,128)(2,1)S(1)}, bf16[2,512,128]{1,2,0:T(8,128)(2,1)S(1)}, u32[]{:S(2)}, u32[]{:S(2)}) collective-permute-start(bf16[2,512,128]{1,2,0:T(8,128)(2,1)S(1)} %copy.31), channel_id=1, source_target_pairs={{0,4},{1,5},{2,6},{3,7},{4,0},{5,1},{6,2},{7,3},{8,12},{9,13},{10,... | collective-permute-start | bytes 786440 | tf_op jit(solution)/shard_map/ppermute | solution.py:12
  15.7 11.4 %collective-permute-start = (bf16[2,512,128]{1,2,0:T(8,128)(2,1)S(1)}, bf16[2,512,128]{1,2,0:T(8,128)(2,1)S(1)}, u32[]{:S(2)}, u32[]{:S(2)}) collective-permute-start(bf16[2,512,128]{1,2,0:T(8,128)(2,1)S(1)} %copy.29), channel_id=1, source_target_pairs={{0,1},{1,0},{2,3},{3,2},{4,5},{5,4},{6,7},{7,6},{8,9},{9,8},{10,11... | collective-permute-start | bytes 786440 | tf_op jit(solution)/shard_map/ppermute | solution.py:12
  17.6 555.2 %copy-start.25 = (pred[2]{0:T(512)(128)(4,1)}, pred[2]{0:T(512)(128)(4,1)S(1)}, u32[]{:S(2)}) copy-start(pred[2]{0:T(512)(128)(4,1)S(1)} %get-tuple-element.18) | copy-start | bytes 10
  17.6 555.2 %copy-start.27 = (pred[2]{0:T(512)(128)(4,1)}, pred[2]{0:T(512)(128)(4,1)S(1)}, u32[]{:S(2)}) copy-start(pred[2]{0:T(512)(128)(4,1)S(1)} %get-tuple-element.20) | copy-start | bytes 10
  17.6 555.1 %copy-start.29 = (pred[2]{0:T(512)(128)(4,1)}, pred[2]{0:T(512)(128)(4,1)S(1)}, u32[]{:S(2)}) copy-start(pred[2]{0:T(512)(128)(4,1)S(1)} %get-tuple-element.24) | copy-start | bytes 10
  17.7 555.1 %copy-start.30 = (pred[2]{0:T(512)(128)(4,1)}, pred[2]{0:T(512)(128)(4,1)S(1)}, u32[]{:S(2)}) copy-start(pred[2]{0:T(512)(128)(4,1)S(1)} %get-tuple-element.22) | copy-start | bytes 10
  27.1 272.6 %copy-start.3 = (f32[2,512,128]{1,2,0:T(8,128)}, f32[2,512,128]{1,2,0:T(8,128)S(1)}, u32[]{:S(2)}) copy-start(f32[2,512,128]{1,2,0:T(8,128)S(1)} %convert_subtract_fusion.1) | copy-start | bytes 1572868
  27.9 271.8 %copy-start.4 = (f32[2,512,128]{1,2,0:T(8,128)}, f32[2,512,128]{1,2,0:T(8,128)S(1)}, u32[]{:S(2)}) copy-start(f32[2,512,128]{1,2,0:T(8,128)S(1)} %convert_subtract_fusion.3) | copy-start | bytes 1572868
  29.8 146.0 %copy-start.21 = (f32[8,1024]{1,0:T(8,128)S(1)}, f32[8,1024]{1,0:T(8,128)}, u32[]{:S(2)}) copy-start(f32[8,1024]{1,0:T(8,128)} %param.14) | copy-start | bytes 98308
  29.8 480.9 %all-reduce.7.cloned.1.call-start = ((), (), s32[]{:S(2)}) async-start(), calls=%async_computation.1 | async-start | bytes 1048576 | tf_op jit(solution)/shard_map/psum | solution.py:57
  214.9 1.3 copy-start.6
  217.2 2.4 collective-permute-start.4
  217.4 7.9 collective-permute-start.7
  217.4 10.3 %collective-permute-start.6 = (bf16[2,512,128]{1,2,0:T(8,128)(2,1)}, bf16[2,512,128]{1,2,0:T(8,128)(2,1)S(1)}, u32[]{:S(2)}, u32[]{:S(2)}) collective-permute-start(bf16[2,512,128]{1,2,0:T(8,128)(2,1)} %get-tuple-element.48), channel_id=1, source_target_pairs={{0,4},{1,5},{2,6},{3,7},{4,0},{5,1},{6,2},{7,3},{8,12},{9,13},{10,... | collective-permute-start | bytes 786440 | tf_op jit(solution)/shard_map/ppermute | solution.py:12
  218.5 12.4 %collective-permute-start.5 = (bf16[2,512,128]{1,2,0:T(8,128)(2,1)}, bf16[2,512,128]{1,2,0:T(8,128)(2,1)S(1)}, u32[]{:S(2)}, u32[]{:S(2)}) collective-permute-start(bf16[2,512,128]{1,2,0:T(8,128)(2,1)} %get-tuple-element.49), channel_id=1, source_target_pairs={{0,2},{1,3},{2,0},{3,1},{4,6},{5,7},{6,4},{7,5},{8,10},{9,11},{10,... | collective-permute-start | bytes 786440 | tf_op jit(solution)/shard_map/ppermute | solution.py:12
  235.1 64.6 %copy-start.8 = (f32[2,512,128]{1,2,0:T(8,128)}, f32[2,512,128]{1,2,0:T(8,128)S(1)}, u32[]{:S(2)}) copy-start(f32[2,512,128]{1,2,0:T(8,128)S(1)} %get-tuple-element.42) | copy-start | bytes 1572868
  235.1 64.6 %copy-start.9 = (f32[2,512,128]{1,2,0:T(8,128)}, f32[2,512,128]{1,2,0:T(8,128)S(1)}, u32[]{:S(2)}) copy-start(f32[2,512,128]{1,2,0:T(8,128)S(1)} %get-tuple-element.43) | copy-start | bytes 1572868
  299.7 340.6 %copy-start.23 = (f32[128]{0:T(128)}, f32[128]{0:T(128)S(1)}, u32[]{:S(2)}) copy-start(f32[128]{0:T(128)S(1)} %div.15) | copy-start | bytes 1540
  368.5 496.3 %all-reduce.9.cloned.1.call-start = ((), (), s32[]{:S(2)}) async-start(), calls=%async_computation.2 | async-start | bytes 1048576 | tf_op jit(solution)/shard_map/psum | solution.py:57
  549.8 1.3 copy-start.7
  552.1 2.2 collective-permute-start.8
  552.3 7.9 collective-permute-start.11
  552.3 12.1 %collective-permute-start.10 = (bf16[2,512,128]{1,2,0:T(8,128)(2,1)}, bf16[2,512,128]{1,2,0:T(8,128)(2,1)}, u32[]{:S(2)}, u32[]{:S(2)}) collective-permute-start(bf16[2,512,128]{1,2,0:T(8,128)(2,1)} %get-tuple-element.40), channel_id=1, source_target_pairs={{0,4},{1,5},{2,6},{3,7},{4,0},{5,1},{6,2},{7,3},{8,12},{9,13},{10,... | collective-permute-start | bytes 786440 | tf_op jit(solution)/shard_map/ppermute | solution.py:12
  553.4 15.1 %collective-permute-start.9 = (bf16[2,512,128]{1,2,0:T(8,128)(2,1)}, bf16[2,512,128]{1,2,0:T(8,128)(2,1)}, u32[]{:S(2)}, u32[]{:S(2)}) collective-permute-start(bf16[2,512,128]{1,2,0:T(8,128)(2,1)} %get-tuple-element.41), channel_id=1, source_target_pairs={{0,2},{1,3},{2,0},{3,1},{4,6},{5,7},{6,4},{7,5},{8,10},{9,11},{10,... | collective-permute-start | bytes 786440 | tf_op jit(solution)/shard_map/ppermute | solution.py:12
  575.6 1.3 copy-start.20
  640.3 3.7 copy-start.31
  717.9 2.0 copy-start.34
  719.9 1.3 copy-start.1
  904.0 1.3 copy-start.5
  906.3 2.2 collective-permute-start.12
  906.5 7.9 collective-permute-start.15
  906.5 12.1 %collective-permute-start.14 = (bf16[2,512,128]{1,2,0:T(8,128)(2,1)}, bf16[2,512,128]{1,2,0:T(8,128)(2,1)}, u32[]{:S(2)}, u32[]{:S(2)}) collective-permute-start(bf16[2,512,128]{1,2,0:T(8,128)(2,1)} %get-tuple-element.32), channel_id=1, source_target_pairs={{0,4},{1,5},{2,6},{3,7},{4,0},{5,1},{6,2},{7,3},{8,12},{9,13},{10,... | collective-permute-start | bytes 786440 | tf_op jit(solution)/shard_map/ppermute | solution.py:12
  907.6 15.1 %collective-permute-start.13 = (bf16[2,512,128]{1,2,0:T(8,128)(2,1)}, bf16[2,512,128]{1,2,0:T(8,128)(2,1)S(1)}, u32[]{:S(2)}, u32[]{:S(2)}) collective-permute-start(bf16[2,512,128]{1,2,0:T(8,128)(2,1)} %get-tuple-element.33), channel_id=1, source_target_pairs={{0,2},{1,3},{2,0},{3,1},{4,6},{5,7},{6,4},{7,5},{8,10},{9,11},{10,... | collective-permute-start | bytes 786440 | tf_op jit(solution)/shard_map/ppermute | solution.py:12
  918.5 7.5 copy-start.26
  918.5 7.5 copy-start.28
  926.0 4.3 copy-start.2
  929.0 1.1 copy-start.15
  929.0 1.3 copy-start.16
  930.4 63.3 %copy-start.35 = (f32[128]{0:T(128)S(1)}, f32[128]{0:T(128)}, u32[]{:S(2)}) copy-start(f32[128]{0:T(128)} %copy-done.34) | copy-start | bytes 1540
  930.4 63.3 %copy-start.24 = (f32[128]{0:T(128)S(1)}, f32[128]{0:T(128)}, u32[]{:S(2)}) copy-start(f32[128]{0:T(128)} %copy-done.23) | copy-start | bytes 1540
  930.4 63.3 %copy-start.32 = (f32[128]{0:T(128)S(1)}, f32[128]{0:T(128)}, u32[]{:S(2)}) copy-start(f32[128]{0:T(128)} %copy-done.31) | copy-start | bytes 1540
  998.8 3.0 copy-start.12
  (7 other events, 6.4 us)
Sparse Core Ops, SparseCore 0:
  29.9 145.7 all-reduce.4
  368.7 141.9 all-reduce.6
  723.2 141.5 all-reduce.8
where the time goes:
time: 1020 us; the launch traced here: 1010 us
  blocking collectives  431 us (42%)
  waiting for transfers between devices  409 us (40%)
  matrix products  57.6 us (6%)
  local copies, waits for them, and re-layouts  45.3 us (4%)
  other arithmetic  38 us (4%)
  starting transfers between devices  15.1 us (1%)
  between operations  14.6 us (1%)
    psum x3, waiting for transfers between devices, apply_operator(): coarse_rhs = lax.psum(coarse_part, 'sub')  391 us
    psum x3, blocking collectives, squares(): return lax.psum(jnp.sum(residual * residual, axis=(0, 1)), 'sub')  200 us
    psum x2, blocking collectives, shards(): curvature = lax.psum(jnp.sum(direction * applied, axis=(0, 1)), 'sub')  126 us
    all_gather x3, blocking collectives, apply_operator(): coarse_sol = lax.all_gather(solved_rows, 'sub', axis=0, tiled=True)  104 us
    dot_general x3, matrix products, apply_operator(): jnp.einsum('sij,sjr->sir', flexibility, rounded, preferred_element_type=j...  38.9 us
    gather x12, local copies, waits for them, and re-layouts, field_jump(): partner = jnp.take(received, adjacency[:, face_round] % sub_count, axis=0)  24.8 us
  transfers between devices with their start and end apart: 19, of which 8 were waited for; matrix products, arithmetic and copies ran while one was open for 7% of the time, Pallas kernels for 0%

commit v1 on v0

v1 whole, which is shorter than its diff:
```python
import jax
import jax.numpy as jnp
from jax import lax
from jax.experimental import pallas as pl
from jax.experimental.pallas import tpu as pltpu
from jax.sharding import PartitionSpec as P

ITERS = 3
FACES = 4
NF = 512
NI = 2048
NC = 16
LOADS = 128
NCG = 1024
BLK = 128
ROWS = BLK + 8
FACE_ORDER = (2, 1, 3, 0)
ARRIVAL = (0, 3, 1, 2)
MESH = pl.DeviceIdType.MESH
F32 = jnp.float32
BF16 = jnp.bfloat16


def flip(index, mask):
    result = index
    bit = 1
    while bit <= mask:
        if mask & bit:
            result = result + bit * (1 - 2 * lax.rem(lax.div(index, bit), 2))
        bit *= 2
    return result


def dot(a, b):
    return jnp.dot(a, b, preferred_element_type=F32)


def sum_rows(gamma, delta):
    row = lax.broadcasted_iota(jnp.int32, (8, LOADS), 0)
    return jnp.where(row == 0, gamma, jnp.where(row == 1, delta, 0.0))


def pick_row(tile, index):
    row = lax.broadcasted_iota(jnp.int32, (8, LOADS), 0)
    return jnp.sum(jnp.where(row == index, tile, 0.0), axis=0, keepdims=True)


def halves(value):
    high = value.astype(BF16)
    return high, (value - high.astype(F32)).astype(BF16)


def kernel(
    adj_ref, ids_ref, cinv_ref, bc_ref, gap_hbm, flex_hbm,
    mult_hbm, res_hbm,
    fv, gapv, rv, pv, uv, xv, frv, rb, frecv, fsend,
    cg, cex, oh, oht, bct, idrecv, brecv,
    s1s, s1r, s2, s3, s4, rb2, yb, cv,
    load_sem, send0, recv0, sendf, recvf, send1, recv1, send2, recv2, send3, recv3, send4, recv4,
):
    me = lax.axis_index("sub")
    core = lax.rem(me, 2)
    yi = lax.rem(lax.div(me, 2), 4)
    zi = lax.rem(lax.div(me, 8), 4)
    xi = lax.div(me, 32)
    chip = lax.div(me, 2)
    grp = xi * 2 + core

    def grp_mask(k):
        return (k // 2) * 32 + (k % 2)

    def remote(src, dst, send, recv, mask):
        return pltpu.make_async_remote_copy(
            src_ref=src, dst_ref=dst, send_sem=send, recv_sem=recv,
            device_id=(flip(me, mask),), device_id_type=MESH,
        )

    barrier = pltpu.get_barrier_semaphore()
    masks = [grp_mask(k) for k in range(1, 8)] + [8, 16, 24, 2, 4, 6]
    for mask in masks:
        pl.semaphore_signal(barrier, inc=1, device_id=(flip(me, mask),), device_id_type=MESH)
    pl.semaphore_wait(barrier, len(masks))

    def gap_copy(f):
        return remote(gap_hbm.at[:, pl.ds(f * NF, NF), :], frecv.at[0, f], sendf.at[0, f], recvf.at[0, f], 1 << f)

    for f in FACE_ORDER:
        gap_copy(f).start()
    gap_load = pltpu.make_async_copy(gap_hbm, gapv, load_sem.at[8])
    gap_load.start()

    setup = []
    core_copy = remote(cinv_ref, cex, send0.at[0], recv0.at[0], 1)
    core_copy.start()
    for f in range(FACES):
        id_copy = remote(ids_ref, idrecv.at[f], send0.at[1 + f], recv0.at[1 + f], 1 << f)
        b_copy = remote(
            bc_ref.at[:, :, pl.ds(f * NF, NF)], brecv.at[f], send0.at[5 + f], recv0.at[5 + f], 1 << f
        )
        id_copy.start()
        b_copy.start()
        setup.append((id_copy, b_copy))

    flex_loads = []
    for s in range(2):
        for f in range(FACES):
            load = pltpu.make_async_copy(
                flex_hbm.at[s, pl.ds(f * NF, NF)], fv.at[s, pl.ds(f * NF, NF)], load_sem.at[s * FACES + f]
            )
            load.start()
            flex_loads.append(load)

    def c_rows(rows, count):
        return cg.at[core, pl.ds(pl.multiple_of(rows, 16), count)]

    def c_stage(base, rows, count, unit):
        part = c_rows(rows, count)
        return [remote(part, part, send0.at[base + k], recv0.at[base + k], unit * k) for k in range(1, 4)]

    core_copy.wait_recv()
    own = cinv_ref[...]
    other = cex[...]
    even = jnp.where(core == 0, own, other)
    odd = jnp.where(core == 0, other, own)
    both = jnp.concatenate([even, odd], axis=0)
    half = jnp.where(core == 0, both[:, : NCG // 2], both[:, NCG // 2 :])
    c_rows(chip * 16, 16)[...] = half.astype(BF16)
    stage_y = c_stage(8, chip * 16, 16, 2)
    for copy in stage_y:
        copy.start()

    lane = lax.broadcasted_iota(jnp.int32, (NC, LOADS), 1)

    def one_hot(ids):
        return [jnp.where(ids == lane + b * LOADS, 1.0, 0.0).astype(F32) for b in range(NCG // LOADS)]

    zeros64 = jnp.zeros((64, LOADS), F32)
    hots = [one_hot(ids_ref[s]) for s in range(2)]
    for b in range(NCG // LOADS):
        tile = jnp.concatenate([hots[0][b], hots[1][b]], axis=0)
        oh[0:32, b * LOADS : (b + 1) * LOADS] = tile.astype(BF16)
        oht[b * LOADS : (b + 1) * LOADS, :] = jnp.concatenate([tile, tile, zeros64], axis=0).T.astype(BF16)

    for copy in stage_y:
        copy.wait_recv()
    stage_z = c_stage(12, lax.div(chip, 4) * 64, 64, 8)
    for copy in stage_z:
        copy.start()

    flags = [[lax.rem(adj_ref[s, f], 2) == 1 for f in range(FACES)] for s in range(2)]
    for f in range(FACES):
        id_copy, b_copy = setup[f]
        id_copy.wait_recv()
        hots = [one_hot(idrecv[f, s]) for s in range(2)]
        for b in range(NCG // LOADS):
            tile = jnp.concatenate([hots[0][b], hots[1][b]], axis=0)
            oh[32 + 32 * f : 64 + 32 * f, b * LOADS : (b + 1) * LOADS] = tile.astype(BF16)
        b_copy.wait_recv()
        for s in range(2):
            for q in range(NF // LOADS):
                cols = slice(q * LOADS, (q + 1) * LOADS)
                mine = bc_ref[s, :, f * NF + q * LOADS : f * NF + (q + 1) * LOADS].astype(F32)
                theirs = jnp.where(flags[s][f], brecv[f, 1, :, cols].astype(F32), brecv[f, 0, :, cols].astype(F32))
                tile = jnp.concatenate([mine, -theirs, mine, -theirs, zeros64], axis=0)
                bct[s, f, cols, :] = tile.T.astype(BF16)

    for copy in stage_z:
        copy.wait_recv()
    stage_x = c_stage(16, xi * 256, 256, 32)
    for copy in stage_x:
        copy.start()
    whole_c = cg.at[core]
    sibling = remote(whole_c, whole_c, send0.at[20], recv0.at[20], 1)

    def clear(i, carry):
        rows = pl.ds(pl.multiple_of(i * 64, 64), 64)
        for s in range(2):
            for ref in (pv, uv, xv):
                ref[s, rows, :] = jnp.zeros((64, LOADS), F32)
        return carry

    lax.fori_loop(0, NI // 64, clear, 0)

    gap_load.wait()
    for f in ARRIVAL:
        gap_copy(f).wait_recv()
        for s in range(2):

            def first(i, carry, s=s, f=f):
                rows = pl.ds(pl.multiple_of(f * NF + i * 128, 128), 128)
                here = pl.ds(pl.multiple_of(i * 128, 128), 128)
                mine = gapv[s, rows, :].astype(F32)
                theirs = jnp.where(
                    flags[s][f], frecv[0, f, 1, here, :].astype(F32), frecv[0, f, 0, here, :].astype(F32)
                )
                value = mine - theirs
                rv[s, rows, :] = value
                rb[s, rows, :] = value.astype(BF16)
                return carry

            lax.fori_loop(0, NF // 128, first, 0)
    for load in flex_loads:
        load.wait()

    def face_copy(k, f):
        return remote(fsend.at[k, f], frecv.at[k + 1, f], sendf.at[k + 1, f], recvf.at[k + 1, f], 1 << f)

    def s1_copy(k, m):
        return remote(
            s1s.at[k, flip_group(m)], s1r.at[k, grp], send1.at[k, m], recv1.at[k, m], grp_mask(m)
        )

    def flip_group(m):
        return flip(grp, m)

    def s2_copy(k, m):
        return remote(s2.at[k, zi], s2.at[k, zi], send2.at[k, m], recv2.at[k, m], 8 * m)

    def s3_copy(k, m):
        return remote(s3.at[k, yi], s3.at[k, yi], send3.at[k, m], recv3.at[k, m], 2 * m)

    def s4_copy(k, m):
        return remote(s4.at[k, grp], s4.at[k, grp], send4.at[k, m], recv4.at[k, m], grp_mask(m))

    zeros64b = jnp.zeros((64, LOADS), BF16)

    def add_slots(ref, k, count):
        total = ref[k, 0].astype(F32)
        for i in range(1, count):
            total = total + ref[k, i].astype(F32)
        return total

    def iteration(k, carry):
        gamma_prev, alpha_prev = carry

        terms = [halves(dot(bc_ref[s], rb[s])) for s in range(2)]
        parts = [terms[0][0], terms[1][0], terms[0][1], terms[1][1], zeros64b]
        dense = dot(oht[...], jnp.concatenate(parts, axis=0))
        s1s[k] = dense.astype(BF16).reshape(8, BLK, LOADS)
        for m in range(1, 8):
            s1_copy(k, m).start()
        s1r[k, grp] = s1s[k, grp]

        gamma = jnp.zeros((1, LOADS), F32)
        delta = jnp.zeros((1, LOADS), F32)
        for f in FACE_ORDER:
            for s in range(2):
                rows = slice(f * NF, (f + 1) * NF)
                frv[s, rows, :] = dot(fv[s, rows, :], rb[s])

                def dots(i, sums, s=s, f=f):
                    at = pl.ds(pl.multiple_of(f * NF + i * 128, 128), 128)
                    fr = frv[s, at, :]
                    r = rv[s, at, :]
                    fsend[k, f, s, pl.ds(pl.multiple_of(i * 128, 128), 128), :] = fr.astype(BF16)
                    g, d = sums
                    return (
                        g + jnp.sum((r * r).reshape(16, 8, LOADS), axis=0),
                        d + jnp.sum((r * fr).reshape(16, 8, LOADS), axis=0),
                    )

                g8, d8 = lax.fori_loop(
                    0, NF // 128, dots, (jnp.zeros((8, LOADS), F32), jnp.zeros((8, LOADS), F32))
                )
                gamma = gamma + jnp.sum(g8, axis=0, keepdims=True)
                delta = delta + jnp.sum(d8, axis=0, keepdims=True)
            face_copy(k, f).start()

        for m in range(1, 8):
            s1_copy(k, m).wait_recv()
        s2[k, zi, :BLK, :] = add_slots(s1r, k, 8)
        s2[k, zi, BLK:, :] = sum_rows(gamma, delta)
        for m in range(1, 4):
            s2_copy(k, m).start()

        @pl.when(k == 0)
        def _():
            for copy in stage_x:
                copy.wait_recv()
            sibling.start()

        for m in range(1, 4):
            s2_copy(k, m).wait_recv()
        s3[k, yi] = add_slots(s2, k, 4)
        for m in range(1, 4):
            s3_copy(k, m).start()
        for m in range(1, 4):
            s3_copy(k, m).wait_recv()
        s4[k, grp] = add_slots(s3, k, 4)
        for m in range(1, 8):
            s4_copy(k, m).start()

        @pl.when(k == 0)
        def _():
            sibling.wait_recv()

        for m in range(1, 8):
            s4_copy(k, m).wait_recv()

        for j in range(8):
            rows = slice(j * BLK, (j + 1) * BLK)
            high, low = halves(s4[k, j, :BLK, :])
            rb2[rows, :LOADS] = high
            rb2[rows, LOADS:] = low
        quad = jnp.zeros((1, LOADS), F32)
        for j in range(8):
            rows = slice(j * BLK, (j + 1) * BLK)
            y = dot(cg[0, rows, :], rb2[: NCG // 2, :]) + dot(cg[1, rows, :], rb2[NCG // 2 :, :])
            y = y[:, :LOADS] + y[:, LOADS:]
            quad = quad + jnp.sum(y * s4[k, j, :BLK, :], axis=0, keepdims=True)
            high, low = halves(y)
            yb[rows, :LOADS] = high
            yb[rows, LOADS:] = low
        tile = s4[k, 0, BLK:, :]
        for j in range(1, 8):
            tile = tile + s4[k, j, BLK:, :]
        gamma = pick_row(tile, 0)
        delta = pick_row(tile, 1)
        picked = dot(oh[...], yb[...])
        cv[...] = picked[:, :LOADS] + picked[:, LOADS:]

        beta = jnp.where(k > 0, gamma / gamma_prev, 0.0)
        alpha = gamma / (2.0 * (delta + quad) - jnp.where(k > 0, beta * gamma / alpha_prev, 0.0))

        for f in ARRIVAL:
            face_copy(k, f).wait_recv()
            for s in range(2):
                theirs = jnp.where(
                    flags[s][f],
                    cv[32 + 32 * f + 16 : 64 + 32 * f, :],
                    cv[32 + 32 * f : 48 + 32 * f, :],
                )
                mine_high, mine_low = halves(cv[16 * s : 16 * s + 16, :])
                high, low = halves(theirs)
                cc = jnp.concatenate([mine_high, high, mine_low, low, zeros64b], axis=0)

                def update(i, carry, s=s, f=f, cc=cc):
                    rows = pl.ds(pl.multiple_of(f * NF + i * 128, 128), 128)
                    here = pl.ds(pl.multiple_of(i * 128, 128), 128)
                    coarse = dot(bct[s, f, here, :], cc)
                    received = jnp.where(
                        flags[s][f],
                        frecv[k + 1, f, 1, here, :].astype(F32),
                        frecv[k + 1, f, 0, here, :].astype(F32),
                    )
                    u = frv[s, rows, :] - received + coarse + beta * uv[s, rows, :]
                    uv[s, rows, :] = u
                    r = rv[s, rows, :]
                    p = r + beta * pv[s, rows, :]
                    pv[s, rows, :] = p
                    xv[s, rows, :] = xv[s, rows, :] + alpha * p
                    r = r - alpha * u
                    rv[s, rows, :] = r
                    rb[s, rows, :] = r.astype(BF16)
                    return carry

                lax.fori_loop(0, NF // 128, update, 0)

        for f in range(FACES):
            face_copy(k, f).wait_send()
        for m in range(1, 8):
            s1_copy(k, m).wait_send()
            s4_copy(k, m).wait_send()
        for m in range(1, 4):
            s2_copy(k, m).wait_send()
            s3_copy(k, m).wait_send()
        return gamma, alpha

    ones = jnp.ones((1, LOADS), F32)
    lax.fori_loop(0, ITERS, iteration, (ones, ones))

    out_mult = pltpu.make_async_copy(xv, mult_hbm, load_sem.at[9])
    out_res = pltpu.make_async_copy(rv, res_hbm, load_sem.at[10])
    out_mult.start()
    out_res.start()
    for f in range(FACES):
        gap_copy(f).wait_send()
        setup[f][0].wait_send()
        setup[f][1].wait_send()
    core_copy.wait_send()
    sibling.wait_send()
    for copy in stage_y + stage_z + stage_x:
        copy.wait_send()
    out_mult.wait()
    out_res.wait()


def shards(gap_loads, flexibility, corner_coupling, corner_ids, coarse_inverse, adjacency):
    ids = jnp.broadcast_to(corner_ids[:, :, None], corner_ids.shape + (LOADS,))
    field = jax.ShapeDtypeStruct((2, NI, LOADS), F32)
    vmem = pl.BlockSpec(memory_space=pltpu.VMEM)
    hbm = pl.BlockSpec(memory_space=pl.ANY)
    dma = pltpu.SemaphoreType.DMA
    return pl.pallas_call(
        kernel,
        out_shape=(field, field),
        in_specs=[pl.BlockSpec(memory_space=pltpu.SMEM), vmem, vmem, vmem, hbm, hbm],
        out_specs=(hbm, hbm),
        scratch_shapes=[
            pltpu.VMEM((2, NI, NI), BF16),
            pltpu.VMEM((2, NI, LOADS), BF16),
            pltpu.VMEM((2, NI, LOADS), F32),
            pltpu.VMEM((2, NI, LOADS), F32),
            pltpu.VMEM((2, NI, LOADS), F32),
            pltpu.VMEM((2, NI, LOADS), F32),
            pltpu.VMEM((2, NI, LOADS), F32),
            pltpu.VMEM((2, NI, LOADS), BF16),
            pltpu.VMEM((ITERS + 1, FACES, 2, NF, LOADS), BF16),
            pltpu.VMEM((ITERS, FACES, 2, NF, LOADS), BF16),
            pltpu.VMEM((2, NCG, NCG // 2), BF16),
            pltpu.VMEM((8, NCG), F32),
            pltpu.VMEM((160, NCG), BF16),
            pltpu.VMEM((NCG, LOADS), BF16),
            pltpu.VMEM((2, FACES, NF, LOADS), BF16),
            pltpu.VMEM((FACES, 2, NC, LOADS), jnp.int32),
            pltpu.VMEM((FACES, 2, NC, NF), BF16),
            pltpu.VMEM((ITERS, 8, BLK, LOADS), BF16),
            pltpu.VMEM((ITERS, 8, BLK, LOADS), BF16),
            pltpu.VMEM((ITERS, 4, ROWS, LOADS), F32),
            pltpu.VMEM((ITERS, 4, ROWS, LOADS), F32),
            pltpu.VMEM((ITERS, 8, ROWS, LOADS), F32),
            pltpu.VMEM((NCG, 2 * LOADS), BF16),
            pltpu.VMEM((NCG, 2 * LOADS), BF16),
            pltpu.VMEM((160, LOADS), F32),
            dma((12,)),
            dma((21,)),
            dma((21,)),
            dma((ITERS + 1, FACES)),
            dma((ITERS + 1, FACES)),
            dma((ITERS, 8)),
            dma((ITERS, 8)),
            dma((ITERS, 4)),
            dma((ITERS, 4)),
            dma((ITERS, 4)),
            dma((ITERS, 4)),
            dma((ITERS, 8)),
            dma((ITERS, 8)),
        ],
        compiler_params=pltpu.CompilerParams(
            collective_id=0, has_side_effects=True, vmem_limit_bytes=60 * 1024 * 1024
        ),
    )(adjacency, ids, coarse_inverse, corner_coupling, gap_loads, flexibility)


def solution(mesh):
    return jax.shard_map(
        shards,
        mesh=mesh,
        in_specs=(
            P("sub", None, None),
            P("sub", None, None),
            P("sub", None, None),
            P("sub", None),
            P("sub", None),
            P("sub", None),
        ),
        out_specs=(P("sub", None, None), P("sub", None, None)),
        check_vma=False,
    )
```

time: 1020 us -> 155 us (0.15)
  blocking collectives: 431 us -> 0 us
  waiting for transfers between devices: 409 us -> 0 us
  Pallas kernels: 0 us -> 149 us
  matrix products: 57.6 us -> 0 us
  local copies, waits for them, and re-layouts: 45.3 us -> 5.87 us
  other arithmetic: 38 us -> 0 us
  starting transfers between devices: 15.1 us -> 0 us
  between operations: 14.6 us -> 0.65 us
    psum x3 -> x0, waiting for transfers between devices: 391 us -> none  [apply_operator(): coarse_rhs = lax.psum(coarse_part, 'sub')]
    psum x5 -> x0, blocking collectives: 326 us -> none  [the longest x3 200 us: squares(): return lax.psum(jnp.sum(residual * residual, axis=(0, 1)), 'sub')]
    pallas_call x0 -> x1, Pallas kernels: none -> 149 us  [shards(): pl.pallas_call(kernel, out_shape=(field, field), in_specs=[pl.BlockSpec(m...]
    all_gather x3 -> x0, blocking collectives: 104 us -> none  [apply_operator(): coarse_sol = lax.all_gather(solved_rows, 'sub', axis=0, tiled=True)]
    dot_general x18 -> x0, matrix products: 57.6 us -> none  [the longest x3 38.9 us: apply_operator(): jnp.einsum('sij,sjr->sir', flexibility, rounded, preferred_element_type=j...]
    gather x16 -> x0, local copies, waits for them, and re-layouts: 27.1 us -> none  [the longest x12 24.8 us: field_jump(): partner = jnp.take(received, adjacency[:, face_round] % sub_count, axis=0)]
    ppermute x16 -> x0, waiting for transfers between devices: 18.3 us -> none  [swapped(): return lax.ppermute(value, axis, pairs)]
    ppermute x16 -> x0, starting transfers between devices: 14.9 us -> none  [swapped(): return lax.ppermute(value, axis, pairs)]
  transfers between devices with their start and end apart: 19 -> 0, of which waited for: 8 -> 0; matrix products, arithmetic and copies ran while one was open for 7% -> 0% of each run, Pallas kernels for 0% -> 0%
where the time goes in v1:
time: 155 us
  Pallas kernels  149 us (96%)
  local copies, waits for them, and re-layouts  5.87 us (4%)
    pallas_call x1, Pallas kernels, shards(): pl.pallas_call(kernel, out_shape=(field, field), in_specs=[pl.BlockSpec(m...  149 us
    unnamed x4, local copies, waits for them, and re-layouts  4.52 us

profile of v1, /device:TPU:1, one launch (start us, length us, event | category | flops | bytes accessed | tf_op | source)
XLA Modules:
  0.0 155.2 jit_solution(13586994655742528117)
XLA Ops:
  0.6 1.4 broadcast_in_dim.2.ids_ref
  2.0 148.7 %shard_map.77 = (f32[2,2048,128]{2,1,0:T(8,128)}, f32[2,2048,128]{2,1,0:T(8,128)}) custom-call(s32[2,4]{1,0:T(2,128)} %adj_ref.1, s32[2,16,128]{2,1,0:T(8,128)} %broadcast_in_dim.2.ids_ref, f32[8,1024]{1,0:T(8,128)} %cinv_ref.1, bf16[2,16,2048]{2,1,0:T(8,128)(2,1)} %bc_ref.1, bf16[2,2048,128]{2,1,0:T(8,128)(2,1)} %gap_hbm.1, bf16[2,2048,2048]{2,1,0:T(8,128)(2,1)} %flex_hbm.1), custom_call_target="tpu_custom_call" | custom-call | tf_op jit(solution)/shard_map/pallas_call | solution.py:394
  150.7 0.0 copy-start
  150.7 3.2 %copy.10 = f32[2,2048,128]{2,1,0:T(8,128)} copy(f32[2,2048,128]{2,1,0:T(8,128)} %get-tuple-element.4) | data formatting | bytes 4194304
  153.9 0.0 copy-done
  153.9 1.3 copy.11
Async XLA Ops:
  150.7 3.2 %copy-start = (f32[2,2048,128]{2,1,0:T(8,128)S(1)}, f32[2,2048,128]{2,1,0:T(8,128)}, u32[]{:S(2)}) copy-start(f32[2,2048,128]{2,1,0:T(8,128)} %get-tuple-element.5) | copy-start | bytes 6291460

commit v2 on v1

v2 whole, which is shorter than its diff:
```python
import jax
import jax.numpy as jnp
from jax import lax
from jax.experimental import pallas as pl
from jax.experimental.pallas import tpu as pltpu
from jax.sharding import PartitionSpec as P

ITERS = 3
FACES = 4
NF = 512
NI = 2048
NC = 16
LOADS = 128
NCG = 1024
BLK = 128
ROWS = BLK + 8
HALF = NCG // 2
WIDE = HALF + LOADS
FACE_ORDER = (2, 1, 3, 0)
ARRIVAL = (0, 3, 1, 2)
MESH = pl.DeviceIdType.MESH
F32 = jnp.float32
BF16 = jnp.bfloat16


def flip(index, mask):
    result = index
    bit = 1
    while bit <= mask:
        if mask & bit:
            result = result + bit * (1 - 2 * lax.rem(lax.div(index, bit), 2))
        bit *= 2
    return result


def dot(a, b):
    return jnp.dot(a, b, preferred_element_type=F32)


def sum_rows(gamma, delta):
    row = lax.broadcasted_iota(jnp.int32, (8, LOADS), 0)
    return jnp.where(row == 0, gamma, jnp.where(row == 1, delta, 0.0))


def pick_row(tile, index):
    row = lax.broadcasted_iota(jnp.int32, (8, LOADS), 0)
    return jnp.sum(jnp.where(row == index, tile, 0.0), axis=0, keepdims=True)


def halves(value):
    high = value.astype(BF16)
    return high, (value - high.astype(F32)).astype(BF16)


def kernel(
    adj_ref, ids_ref, cinv_ref, bc_ref, gap_hbm, flex_hbm,
    mult_hbm, res_hbm,
    fv, gapv, rv, pv, uv, xv, frv, rb, frecv, fsend,
    cg, cex, oh, oht, bct, idrecv, brecv,
    s1s, s1r, a1, a2, b1, b2, d1, d2, s4, rb2, yb, cv,
    load_sem, send0, recv0, sendg, recvg, sendf, recvf, send1, recv1,
    senda1, recva1, senda2, recva2, sendb1, recvb1, sendb2, recvb2,
    sendd1, recvd1, sendd2, recvd2, send4, recv4,
):
    me = lax.axis_index("sub")
    core = lax.rem(me, 2)
    zi = lax.rem(lax.div(me, 8), 4)
    xi = lax.div(me, 32)
    chip = lax.div(me, 2)
    grp = lax.rem(me, 8)

    def remote(src, dst, send, recv, mask):
        return pltpu.make_async_remote_copy(
            src_ref=src, dst_ref=dst, send_sem=send, recv_sem=recv,
            device_id=(flip(me, mask),), device_id_type=MESH,
        )

    barrier = pltpu.get_barrier_semaphore()
    masks = [1, 2, 3, 4, 5, 6, 7, 8, 16, 24, 32, 64, 96]
    for mask in masks:
        pl.semaphore_signal(barrier, inc=1, device_id=(flip(me, mask),), device_id_type=MESH)
    pl.semaphore_wait(barrier, len(masks))

    def gap_copy(f, s):
        at = 2 * f + s
        return remote(
            gap_hbm.at[s, pl.ds(f * NF, NF), :], frecv.at[0, f, s], sendg.at[at], recvg.at[at], 1 << f
        )

    core_copy = remote(cinv_ref, cex, send0.at[0], recv0.at[0], 1)
    core_copy.start()
    gap_copy(2, 0).start()
    gap_copy(1, 0).start()
    gap_load = pltpu.make_async_copy(gap_hbm, gapv, load_sem.at[8])
    gap_load.start()

    setup = []
    for f in range(FACES):
        id_copy = remote(ids_ref, idrecv.at[f], send0.at[1 + f], recv0.at[1 + f], 1 << f)
        b_copy = remote(
            bc_ref.at[:, :, pl.ds(f * NF, NF)], brecv.at[f], send0.at[5 + f], recv0.at[5 + f], 1 << f
        )
        setup.append((id_copy, b_copy))

    flex_loads = []
    for s in range(2):
        for f in range(FACES):
            load = pltpu.make_async_copy(
                flex_hbm.at[s, pl.ds(f * NF, NF)], fv.at[s, pl.ds(f * NF, NF)], load_sem.at[s * FACES + f]
            )
            load.start()
            flex_loads.append(load)

    def c_rows(rows, count):
        return cg.at[core, pl.ds(pl.multiple_of(rows, 16), count)]

    def c_stage(base, rows, count, unit):
        part = c_rows(rows, count)
        return [remote(part, part, send0.at[base + k], recv0.at[base + k], unit * k) for k in range(1, 4)]

    core_copy.wait_recv()
    own = cinv_ref[...]
    other = cex[...]
    even = jnp.where(core == 0, own, other)
    odd = jnp.where(core == 0, other, own)
    both = jnp.concatenate([even, odd], axis=0)
    half = jnp.where(core == 0, both[:, :HALF], both[:, HALF:])
    across = lax.broadcasted_iota(jnp.int32, (16, NCG), 1)
    down = lax.broadcasted_iota(jnp.int32, (16, NCG), 0)
    rest = both - both.astype(BF16).astype(F32)
    rest = jnp.sum(jnp.where(across == down + chip * 16, rest, 0.0), axis=1, keepdims=True)
    packed = jnp.concatenate([half, jnp.broadcast_to(rest, (16, LOADS))], axis=1)
    c_rows(chip * 16, 16)[...] = packed.astype(BF16)
    stage_y = c_stage(8, chip * 16, 16, 2)
    for copy in stage_y:
        copy.start()
    for f, s in ((2, 1), (1, 1), (3, 0), (3, 1), (0, 0), (0, 1)):
        gap_copy(f, s).start()
    for id_copy, b_copy in setup:
        id_copy.start()
        b_copy.start()

    lane = lax.broadcasted_iota(jnp.int32, (NC, LOADS), 1)

    def one_hot(ids):
        return [jnp.where(ids == lane + b * LOADS, 1.0, 0.0).astype(F32) for b in range(NCG // LOADS)]

    zeros64 = jnp.zeros((64, LOADS), F32)
    hots = [one_hot(ids_ref[s]) for s in range(2)]
    for b in range(NCG // LOADS):
        tile = jnp.concatenate([hots[0][b], hots[1][b]], axis=0)
        oh[0:32, b * LOADS : (b + 1) * LOADS] = tile.astype(BF16)
        oht[b * LOADS : (b + 1) * LOADS, :] = jnp.concatenate([tile, tile, zeros64], axis=0).T.astype(BF16)

    for copy in stage_y:
        copy.wait_recv()
    stage_z = c_stage(12, lax.div(chip, 4) * 64, 64, 8)
    for copy in stage_z:
        copy.start()

    flags = [[lax.rem(adj_ref[s, f], 2) == 1 for f in range(FACES)] for s in range(2)]
    for f in range(FACES):
        id_copy, b_copy = setup[f]
        id_copy.wait_recv()
        hots = [one_hot(idrecv[f, s]) for s in range(2)]
        for b in range(NCG // LOADS):
            tile = jnp.concatenate([hots[0][b], hots[1][b]], axis=0)
            oh[32 + 32 * f : 64 + 32 * f, b * LOADS : (b + 1) * LOADS] = tile.astype(BF16)
        b_copy.wait_recv()
        for s in range(2):
            for q in range(NF // LOADS):
                cols = slice(q * LOADS, (q + 1) * LOADS)
                mine = bc_ref[s, :, f * NF + q * LOADS : f * NF + (q + 1) * LOADS].astype(F32)
                theirs = jnp.where(flags[s][f], brecv[f, 1, :, cols].astype(F32), brecv[f, 0, :, cols].astype(F32))
                tile = jnp.concatenate([mine, -theirs, mine, -theirs, zeros64], axis=0)
                bct[s, f, cols, :] = tile.T.astype(BF16)

    for copy in stage_z:
        copy.wait_recv()
    stage_x = c_stage(16, xi * 256, 256, 32)
    for copy in stage_x:
        copy.start()
    whole_c = cg.at[core]
    sibling = remote(whole_c, whole_c, send0.at[20], recv0.at[20], 1)

    def clear(i, carry):
        rows = pl.ds(pl.multiple_of(i * 64, 64), 64)
        for s in range(2):
            for ref in (pv, uv, xv):
                ref[s, rows, :] = jnp.zeros((64, LOADS), F32)
        return carry

    lax.fori_loop(0, NI // 64, clear, 0)

    gap_load.wait()
    for f in ARRIVAL:
        gap_copy(f, 0).wait_recv()
        gap_copy(f, 1).wait_recv()
        for s in range(2):
            for i in range(NF // 128):
                rows = slice(f * NF + i * 128, f * NF + i * 128 + 128)
                here = slice(i * 128, i * 128 + 128)
                mine = gapv[s, rows, :].astype(F32)
                theirs = jnp.where(
                    flags[s][f], frecv[0, f, 1, here, :].astype(F32), frecv[0, f, 0, here, :].astype(F32)
                )
                value = mine - theirs
                rv[0, s, rows, :] = value
                rb[s, rows, :] = value.astype(BF16)
    for load in flex_loads:
        load.wait()

    def face_copy(k, f):
        return remote(fsend.at[k, f], frecv.at[k + 1, f], sendf.at[k + 1, f], recvf.at[k + 1, f], 1 << f)

    def s1_copy(k, m):
        return remote(
            s1s.at[k, flip_group(m)], s1r.at[k, grp], send1.at[k, m], recv1.at[k, m], m
        )

    def flip_group(m):
        return flip(grp, m)

    def a1_copy(k, m):
        return remote(a1.at[k, zi], a1.at[k, zi], senda1.at[k, m], recva1.at[k, m], 8 * m)

    def a2_copy(k, m):
        return remote(a2.at[k, xi], a2.at[k, xi], senda2.at[k, m], recva2.at[k, m], 32 * m)

    def b1_copy(k, m):
        return remote(b1.at[k, xi], b1.at[k, xi], sendb1.at[k, m], recvb1.at[k, m], 32 * m)

    def b2_copy(k, m):
        return remote(b2.at[k, zi], b2.at[k, zi], sendb2.at[k, m], recvb2.at[k, m], 8 * m)

    def d1_copy(k, m):
        return remote(d1.at[k, zi], d1.at[k, zi], sendd1.at[k, m], recvd1.at[k, m], 8 * m)

    def d2_copy(k, m):
        return remote(d2.at[k, xi], d2.at[k, xi], sendd2.at[k, m], recvd2.at[k, m], 32 * m)

    def y4_copy(k, m):
        return remote(s4.at[k, grp], s4.at[k, grp], send4.at[k, m], recv4.at[k, m], 2 * m)

    def c4_copy(k, m):
        block = s4.at[k, flip(grp, 2 * m)]
        return remote(block, block, send4.at[k, 4 + m], recv4.at[k, 4 + m], 1)

    zeros64b = jnp.zeros((64, LOADS), BF16)

    def add_slots(ref, k, count):
        total = ref[k, 0].astype(F32)
        for i in range(1, count):
            total = total + ref[k, i].astype(F32)
        return total

    def follow(k, beta, alpha):
        for s in range(2):
            for i in range(NI // 128):
                rows = slice(i * 128, i * 128 + 128)
                p = rv[k, s, rows, :] + beta * pv[s, rows, :]
                pv[s, rows, :] = p
                xv[s, rows, :] = xv[s, rows, :] + alpha * p

    def iteration(k, carry):
        gamma_prev, alpha_prev, beta_prev = carry

        terms = [halves(dot(bc_ref[s], rb[s])) for s in range(2)]
        parts = [terms[0][0], terms[1][0], terms[0][1], terms[1][1], zeros64b]
        s1s[k] = dot(oht[...], jnp.concatenate(parts, axis=0)).astype(BF16).reshape(8, BLK, LOADS)
        for m in range(1, 8):
            s1_copy(k, m).start()
        s1r[k, grp] = s1s[k, grp]

        gamma = jnp.zeros((8, LOADS), F32)
        delta = jnp.zeros((8, LOADS), F32)
        for place, f in enumerate(FACE_ORDER):
            for s in range(2):
                frv[s, f * NF : (f + 1) * NF, :] = dot(fv[s, f * NF : (f + 1) * NF, :], rb[s])
                for i in range(NF // 128):
                    rows = slice(f * NF + i * 128, f * NF + i * 128 + 128)
                    fr = frv[s, rows, :]
                    r = rv[k, s, rows, :]
                    fsend[k, f, s, i * 128 : i * 128 + 128, :] = fr.astype(BF16)
                    gamma = gamma + jnp.sum((r * r).reshape(16, 8, LOADS), axis=0)
                    delta = delta + jnp.sum((r * fr).reshape(16, 8, LOADS), axis=0)
            if f != 3:
                face_copy(k, f).start()
            if place == 1:
                for m in range(1, 8):
                    s1_copy(k, m).wait_recv()
                total = add_slots(s1r, k, 8)
                a1[k, zi] = total[:64]
                b1[k, xi] = total[64:]
                for m in range(1, 4):
                    a1_copy(k, m).start()
                    b1_copy(k, m).start()
        d1[k, zi] = sum_rows(
            jnp.sum(gamma, axis=0, keepdims=True), jnp.sum(delta, axis=0, keepdims=True)
        )
        for m in range(1, 4):
            d1_copy(k, m).start()

        for m in range(1, 4):
            a1_copy(k, m).wait_recv()
            b1_copy(k, m).wait_recv()
        a2[k, xi] = add_slots(a1, k, 4)
        b2[k, zi] = add_slots(b1, k, 4)
        for m in range(1, 4):
            a2_copy(k, m).start()
            b2_copy(k, m).start()
        face_copy(k, 3).start()
        for m in range(1, 4):
            d1_copy(k, m).wait_recv()
        d2[k, xi] = add_slots(d1, k, 4)
        for m in range(1, 4):
            d2_copy(k, m).start()

        @pl.when(k > 0)
        def _():
            follow(k - 1, beta_prev, alpha_prev)

        for m in range(1, 4):
            a2_copy(k, m).wait_recv()
            b2_copy(k, m).wait_recv()
            d2_copy(k, m).wait_recv()
        s4[k, grp, :64, :] = add_slots(a2, k, 4)
        s4[k, grp, 64:BLK, :] = add_slots(b2, k, 4)
        s4[k, grp, BLK:, :] = add_slots(d2, k, 4)
        for m in range(1, 4):
            y4_copy(k, m).start()
        c4_copy(k, 0).start()

        @pl.when(k == 0)
        def _():
            for copy in stage_x:
                copy.wait_recv()
            sibling.start()

        for f in ARRIVAL:
            face_copy(k, f).wait_recv()
            for s in range(2):
                for i in range(NF // 128):
                    rows = slice(f * NF + i * 128, f * NF + i * 128 + 128)
                    here = slice(i * 128, i * 128 + 128)
                    received = jnp.where(
                        flags[s][f],
                        frecv[k + 1, f, 1, here, :].astype(F32),
                        frecv[k + 1, f, 0, here, :].astype(F32),
                    )
                    frv[s, rows, :] = frv[s, rows, :] - received

        for m in range(1, 4):
            y4_copy(k, m).wait_recv()
            c4_copy(k, m).start()

        @pl.when(k == 0)
        def _():
            sibling.wait_recv()

        for m in range(4):
            c4_copy(k, m).wait_recv()

        for j in range(8):
            rows = slice(j * BLK, (j + 1) * BLK)
            high, low = halves(s4[k, j, :BLK, :])
            rb2[rows, :LOADS] = high
            rb2[rows, LOADS:] = low
        quad = jnp.zeros((8, LOADS), F32)
        for j in range(8):
            rows = slice(j * BLK, (j + 1) * BLK)
            rhs = s4[k, j, :BLK, :]
            y = dot(cg[0, rows, :HALF], rb2[:HALF, :]) + dot(cg[1, rows, :HALF], rb2[HALF:, :])
            y = y[:, :LOADS] + y[:, LOADS:] + cg[0, rows, HALF:].astype(F32) * rhs
            quad = quad + jnp.sum((y * rhs).reshape(16, 8, LOADS), axis=0)
            high, low = halves(y)
            yb[rows, :LOADS] = high
            yb[rows, LOADS:] = low
        quad = jnp.sum(quad, axis=0, keepdims=True)
        tile = s4[k, 0, BLK:, :]
        for j in range(1, 8):
            tile = tile + s4[k, j, BLK:, :]
        gamma = pick_row(tile, 0)
        delta = pick_row(tile, 1)
        picked = dot(oh[...], yb[...])
        cv[...] = picked[:, :LOADS] + picked[:, LOADS:]

        beta = jnp.where(k > 0, gamma / gamma_prev, 0.0)
        alpha = gamma / (2.0 * (delta + quad) - jnp.where(k > 0, beta * gamma / alpha_prev, 0.0))

        for f in range(FACES):
            for s in range(2):
                theirs = jnp.where(
                    flags[s][f],
                    cv[32 + 32 * f + 16 : 64 + 32 * f, :],
                    cv[32 + 32 * f : 48 + 32 * f, :],
                )
                mine_high, mine_low = halves(cv[16 * s : 16 * s + 16, :])
                high, low = halves(theirs)
                cc = jnp.concatenate([mine_high, high, mine_low, low, zeros64b], axis=0)
                for i in range(NF // 128):
                    rows = slice(f * NF + i * 128, f * NF + i * 128 + 128)
                    coarse = dot(bct[s, f, i * 128 : i * 128 + 128, :], cc)
                    u = frv[s, rows, :] + coarse + beta * uv[s, rows, :]
                    uv[s, rows, :] = u
                    r = rv[k, s, rows, :] - alpha * u
                    rv[k + 1, s, rows, :] = r
                    rb[s, rows, :] = r.astype(BF16)

        for f in range(FACES):
            face_copy(k, f).wait_send()
            c4_copy(k, f).wait_send()
        for m in range(1, 8):
            s1_copy(k, m).wait_send()
        for m in range(1, 4):
            a1_copy(k, m).wait_send()
            a2_copy(k, m).wait_send()
            b1_copy(k, m).wait_send()
            b2_copy(k, m).wait_send()
            d1_copy(k, m).wait_send()
            d2_copy(k, m).wait_send()
            y4_copy(k, m).wait_send()
        return gamma, alpha, beta

    ones = jnp.ones((1, LOADS), F32)
    _, alpha, beta = lax.fori_loop(0, ITERS, iteration, (ones, ones, ones))

    out_res = pltpu.make_async_copy(rv.at[ITERS], res_hbm, load_sem.at[10])
    out_res.start()
    follow(ITERS - 1, beta, alpha)
    out_mult = pltpu.make_async_copy(xv, mult_hbm, load_sem.at[9])
    out_mult.start()
    for f in range(FACES):
        gap_copy(f, 0).wait_send()
        gap_copy(f, 1).wait_send()
        setup[f][0].wait_send()
        setup[f][1].wait_send()
    core_copy.wait_send()
    sibling.wait_send()
    for copy in stage_y + stage_z + stage_x:
        copy.wait_send()
    out_mult.wait()
    out_res.wait()


def shards(gap_loads, flexibility, corner_coupling, corner_ids, coarse_inverse, adjacency):
    ids = jnp.broadcast_to(corner_ids[:, :, None], corner_ids.shape + (LOADS,))
    field = jax.ShapeDtypeStruct((2, NI, LOADS), F32)
    vmem = pl.BlockSpec(memory_space=pltpu.VMEM)
    hbm = pl.BlockSpec(memory_space=pl.ANY)
    dma = pltpu.SemaphoreType.DMA
    return pl.pallas_call(
        kernel,
        out_shape=(field, field),
        in_specs=[pl.BlockSpec(memory_space=pltpu.SMEM), vmem, vmem, vmem, hbm, hbm],
        out_specs=(hbm, hbm),
        scratch_shapes=[
            pltpu.VMEM((2, NI, NI), BF16),
            pltpu.VMEM((2, NI, LOADS), BF16),
            pltpu.VMEM((ITERS + 1, 2, NI, LOADS), F32),
            pltpu.VMEM((2, NI, LOADS), F32),
            pltpu.VMEM((2, NI, LOADS), F32),
            pltpu.VMEM((2, NI, LOADS), F32),
            pltpu.VMEM((2, NI, LOADS), F32),
            pltpu.VMEM((2, NI, LOADS), BF16),
            pltpu.VMEM((ITERS + 1, FACES, 2, NF, LOADS), BF16),
            pltpu.VMEM((ITERS, FACES, 2, NF, LOADS), BF16),
            pltpu.VMEM((2, NCG, WIDE), BF16),
            pltpu.VMEM((8, NCG), F32),
            pltpu.VMEM((160, NCG), BF16),
            pltpu.VMEM((NCG, LOADS), BF16),
            pltpu.VMEM((2, FACES, NF, LOADS), BF16),
            pltpu.VMEM((FACES, 2, NC, LOADS), jnp.int32),
            pltpu.VMEM((FACES, 2, NC, NF), BF16),
            pltpu.VMEM((ITERS, 8, BLK, LOADS), BF16),
            pltpu.VMEM((ITERS, 8, BLK, LOADS), BF16),
            pltpu.VMEM((ITERS, 4, 64, LOADS), F32),
            pltpu.VMEM((ITERS, 4, 64, LOADS), F32),
            pltpu.VMEM((ITERS, 4, 64, LOADS), F32),
            pltpu.VMEM((ITERS, 4, 64, LOADS), F32),
            pltpu.VMEM((ITERS, 4, 8, LOADS), F32),
            pltpu.VMEM((ITERS, 4, 8, LOADS), F32),
            pltpu.VMEM((ITERS, 8, ROWS, LOADS), F32),
            pltpu.VMEM((NCG, 2 * LOADS), BF16),
            pltpu.VMEM((NCG, 2 * LOADS), BF16),
            pltpu.VMEM((160, LOADS), F32),
            dma((12,)),
            dma((21,)),
            dma((21,)),
            dma((8,)),
            dma((8,)),
            dma((ITERS + 1, FACES)),
            dma((ITERS + 1, FACES)),
            dma((ITERS, 8)),
            dma((ITERS, 8)),
        ]
        + [dma((ITERS, 4))] * 12
        + [dma((ITERS, 8))] * 2,
        compiler_params=pltpu.CompilerParams(
            collective_id=0, has_side_effects=True, vmem_limit_bytes=60 * 1024 * 1024
        ),
    )(adjacency, ids, coarse_inverse, corner_coupling, gap_loads, flexibility)


def solution(mesh):
    return jax.shard_map(
        shards,
        mesh=mesh,
        in_specs=(
            P("sub", None, None),
            P("sub", None, None),
            P("sub", None, None),
            P("sub", None),
            P("sub", None),
            P("sub", None),
        ),
        out_specs=(P("sub", None, None), P("sub", None, None)),
        check_vma=False,
    )
```

time: 155 us -> 115 us (0.74)
  Pallas kernels: 149 us -> 107 us
    pallas_call x1, Pallas kernels: 149 us -> 107 us  [shards(): pl.pallas_call(kernel, out_shape=(field, field), in_specs=[pl.BlockSpec(m...]
where the time goes in v2:
time: 115 us; the launch traced here: 114 us
  Pallas kernels  107 us (93%)
  local copies, waits for them, and re-layouts  5.87 us (5%)
    pallas_call x1, Pallas kernels, shards(): pl.pallas_call(kernel, out_shape=(field, field), in_specs=[pl.BlockSpec(m...  107 us
    unnamed x4, local copies, waits for them, and re-layouts  4.52 us

profile of v2, /device:TPU:1, one launch (start us, length us, event | category | flops | bytes accessed | tf_op | source)
XLA Modules:
  0.0 113.8 jit_solution(3393159857169702049)
XLA Ops:
  0.6 1.4 %broadcast_in_dim.2.ids_ref = s32[2,16,128]{2,1,0:T(8,128)} broadcast(s32[2,16]{1,0:T(2,128)} %param.9), dimensions={0,1} | broadcast | bytes 16512 | tf_op jit(solution)/shard_map/broadcast_in_dim | solution.py:447
  2.0 107.3 %shard_map.77 = (f32[2,2048,128]{2,1,0:T(8,128)}, f32[2,2048,128]{2,1,0:T(8,128)}) custom-call(s32[2,4]{1,0:T(2,128)} %adj_ref.1, s32[2,16,128]{2,1,0:T(8,128)} %broadcast_in_dim.2.ids_ref, f32[8,1024]{1,0:T(8,128)} %cinv_ref.1, bf16[2,16,2048]{2,1,0:T(8,128)(2,1)} %bc_ref.1, bf16[2,2048,128]{2,1,0:T(8,128)(2,1)} %gap_hbm.1, bf16[2,2048,2048]{2,1,0:T(8,128)(2,1)} %flex_hbm.1), custom_call_target="tpu_custom_call" | custom-call | tf_op jit(solution)/shard_map/pallas_call | solution.py:452
  109.3 0.0 copy-start
  109.3 3.2 %copy.10 = f32[2,2048,128]{2,1,0:T(8,128)} copy(f32[2,2048,128]{2,1,0:T(8,128)} %get-tuple-element.4) | data formatting | bytes 4194304
  112.5 0.0 copy-done
  112.5 1.3 %copy.11 = f32[2,2048,128]{2,1,0:T(8,128)} copy(f32[2,2048,128]{2,1,0:T(8,128)S(1)} %copy-done) | data formatting | bytes 4194304
Async XLA Ops:
  109.3 3.2 %copy-start = (f32[2,2048,128]{2,1,0:T(8,128)S(1)}, f32[2,2048,128]{2,1,0:T(8,128)}, u32[]{:S(2)}) copy-start(f32[2,2048,128]{2,1,0:T(8,128)} %get-tuple-element.5) | copy-start | bytes 6291460

commit v3 on v2

--- a/solution.py
+++ b/solution.py
@@ -13,7 +13,6 @@
 LOADS = 128
 NCG = 1024
 BLK = 128
-ROWS = BLK + 8
 HALF = NCG // 2
 WIDE = HALF + LOADS
 FACE_ORDER = (2, 1, 3, 0)
@@ -56,11 +55,11 @@
     adj_ref, ids_ref, cinv_ref, bc_ref, gap_hbm, flex_hbm,
     mult_hbm, res_hbm,
     fv, gapv, rv, pv, uv, xv, frv, rb, frecv, fsend,
-    cg, cex, oh, oht, bct, idrecv, brecv,
-    s1s, s1r, a1, a2, b1, b2, d1, d2, s4, rb2, yb, cv,
+    cg, cex, oh, scat, bct, idg, idz, brecv,
+    s1, a1, a2, b1, b2, d1, d2, d3, s4, rb2, yb, cv,
     load_sem, send0, recv0, sendg, recvg, sendf, recvf, send1, recv1,
     senda1, recva1, senda2, recva2, sendb1, recvb1, sendb2, recvb2,
-    sendd1, recvd1, sendd2, recvd2, send4, recv4,
+    sendd1, recvd1, sendd2, recvd2, sendd3, recvd3, send4, recv4, sendi, recvi,
 ):
     me = lax.axis_index("sub")
     core = lax.rem(me, 2)
@@ -94,13 +93,13 @@
     gap_load = pltpu.make_async_copy(gap_hbm, gapv, load_sem.at[8])
     gap_load.start()
 
-    setup = []
-    for f in range(FACES):
-        id_copy = remote(ids_ref, idrecv.at[f], send0.at[1 + f], recv0.at[1 + f], 1 << f)
-        b_copy = remote(
-            bc_ref.at[:, :, pl.ds(f * NF, NF)], brecv.at[f], send0.at[5 + f], recv0.at[5 + f], 1 << f
-        )
-        setup.append((id_copy, b_copy))
+    id_copies = [
+        remote(ids_ref, idg.at[grp], sendi.at[m], recvi.at[m], m) for m in range(1, 8)
+    ] + [remote(ids_ref, idz, sendi.at[0], recvi.at[0], 8)]
+    b_copies = [
+        remote(bc_ref.at[:, :, pl.ds(f * NF, NF)], brecv.at[f], send0.at[5 + f], recv0.at[5 + f], 1 << f)
+        for f in range(FACES)
+    ]
 
     flex_loads = []
     for s in range(2):
@@ -136,9 +135,9 @@
         copy.start()
     for f, s in ((2, 1), (1, 1), (3, 0), (3, 1), (0, 0), (0, 1)):
         gap_copy(f, s).start()
-    for id_copy, b_copy in setup:
-        id_copy.start()
-        b_copy.start()
+    for copy in id_copies + b_copies:
+        copy.start()
+    idg[grp] = ids_ref[...]
 
     lane = lax.broadcasted_iota(jnp.int32, (NC, LOADS), 1)
 
@@ -146,34 +145,57 @@
         return [jnp.where(ids == lane + b * LOADS, 1.0, 0.0).astype(F32) for b in range(NCG // LOADS)]
 
     zeros64 = jnp.zeros((64, LOADS), F32)
-    hots = [one_hot(ids_ref[s]) for s in range(2)]
-    for b in range(NCG // LOADS):
-        tile = jnp.concatenate([hots[0][b], hots[1][b]], axis=0)
-        oh[0:32, b * LOADS : (b + 1) * LOADS] = tile.astype(BF16)
-        oht[b * LOADS : (b + 1) * LOADS, :] = jnp.concatenate([tile, tile, zeros64], axis=0).T.astype(BF16)
+    flags = [[lax.rem(adj_ref[s, f], 2) == 1 for f in range(FACES)] for s in range(2)]
+
+    def spread(base, ids):
+        hots = [one_hot(ids[s]) for s in range(2)]
+        for b in range(NCG // LOADS):
+            tile = jnp.concatenate([hots[0][b], hots[1][b]], axis=0)
+            oh[base : base + 32, b * LOADS : (b + 1) * LOADS] = tile.astype(BF16)
+
+    def build_scatter():
+        for copy in id_copies:
+            copy.wait_recv()
+        mine = lane + grp * BLK
+        for q in range(2):
+            tiles = [
+                jnp.where(idg[e, s] == mine, 1.0, 0.0).astype(F32)
+                for e in range(4 * q, 4 * q + 4)
+                for s in range(2)
+            ]
+            scat[:, q * LOADS : (q + 1) * LOADS] = jnp.concatenate(tiles, axis=0).T.astype(BF16)
+
+    def build_corners():
+        spread(0, ids_ref)
+        for f in range(3):
+            spread(32 + 32 * f, idg.at[flip(grp, 1 << f)])
+        spread(32 + 32 * 3, idz)
+        for f in range(FACES):
+            b_copies[f].wait_recv()
+            for s in range(2):
+                for q in range(NF // LOADS):
+                    cols = slice(q * LOADS, (q + 1) * LOADS)
+                    mine = bc_ref[s, :, f * NF + q * LOADS : f * NF + (q + 1) * LOADS].astype(F32)
+                    theirs = jnp.where(
+                        flags[s][f], brecv[f, 1, :, cols].astype(F32), brecv[f, 0, :, cols].astype(F32)
+                    )
+                    tile = jnp.concatenate([mine, -theirs, mine, -theirs, zeros64], axis=0)
+                    bct[s, f, cols, :] = tile.T.astype(BF16)
+
+    def clear(i, carry):
+        rows = pl.ds(pl.multiple_of(i * 64, 64), 64)
+        for s in range(2):
+            for ref in (pv, uv, xv):
+                ref[s, rows, :] = jnp.zeros((64, LOADS), F32)
+        return carry
+
+    lax.fori_loop(0, NI // 64, clear, 0)
 
     for copy in stage_y:
         copy.wait_recv()
     stage_z = c_stage(12, lax.div(chip, 4) * 64, 64, 8)
     for copy in stage_z:
         copy.start()
-
-    flags = [[lax.rem(adj_ref[s, f], 2) == 1 for f in range(FACES)] for s in range(2)]
-    for f in range(FACES):
-        id_copy, b_copy = setup[f]
-        id_copy.wait_recv()
-        hots = [one_hot(idrecv[f, s]) for s in range(2)]
-        for b in range(NCG // LOADS):
-            tile = jnp.concatenate([hots[0][b], hots[1][b]], axis=0)
-            oh[32 + 32 * f : 64 + 32 * f, b * LOADS : (b + 1) * LOADS] = tile.astype(BF16)
-        b_copy.wait_recv()
-        for s in range(2):
-            for q in range(NF // LOADS):
-                cols = slice(q * LOADS, (q + 1) * LOADS)
-                mine = bc_ref[s, :, f * NF + q * LOADS : f * NF + (q + 1) * LOADS].astype(F32)
-                theirs = jnp.where(flags[s][f], brecv[f, 1, :, cols].astype(F32), brecv[f, 0, :, cols].astype(F32))
-                tile = jnp.concatenate([mine, -theirs, mine, -theirs, zeros64], axis=0)
-                bct[s, f, cols, :] = tile.T.astype(BF16)
 
     for copy in stage_z:
         copy.wait_recv()
@@ -182,15 +204,6 @@
         copy.start()
     whole_c = cg.at[core]
     sibling = remote(whole_c, whole_c, send0.at[20], recv0.at[20], 1)
-
-    def clear(i, carry):
-        rows = pl.ds(pl.multiple_of(i * 64, 64), 64)
-        for s in range(2):
-            for ref in (pv, uv, xv):
-                ref[s, rows, :] = jnp.zeros((64, LOADS), F32)
-        return carry
-
-    lax.fori_loop(0, NI // 64, clear, 0)
 
     gap_load.wait()
     for f in ARRIVAL:
@@ -214,12 +227,10 @@
         return remote(fsend.at[k, f], frecv.at[k + 1, f], sendf.at[k + 1, f], recvf.at[k + 1, f], 1 << f)
 
     def s1_copy(k, m):
-        return remote(
-            s1s.at[k, flip_group(m)], s1r.at[k, grp], send1.at[k, m], recv1.at[k, m], m
-        )
-
-    def flip_group(m):
-        return flip(grp, m)
+        return remote(s1.at[k, grp], s1.at[k, grp], send1.at[k, m], recv1.at[k, m], m)
+
+    def d3_copy(k, m):
+        return remote(d3.at[k, grp], d3.at[k, grp], sendd3.at[k, m], recvd3.at[k, m], m)
 
     def a1_copy(k, m):
         return remote(a1.at[k, zi], a1.at[k, zi], senda1.at[k, m], recva1.at[k, m], 8 * m)
@@ -247,6 +258,17 @@
         return remote(block, block, send4.at[k, 4 + m], recv4.at[k, 4 + m], 1)
 
     zeros64b = jnp.zeros((64, LOADS), BF16)
+
+    def sent(k):
+        for f in range(FACES):
+            face_copy(k, f).wait_send()
+            c4_copy(k, f).wait_send()
+        for m in range(1, 8):
+            s1_copy(k, m).wait_send()
+            d3_copy(k, m).wait_send()
+        for m in range(1, 4):
+            for copy in (a1_copy, a2_copy, b1_copy, b2_copy, d1_copy, d2_copy, y4_copy):
+                copy(k, m).wait_send()
 
     def add_slots(ref, k, count):
         total = ref[k, 0].astype(F32)
@@ -265,12 +287,9 @@
     def iteration(k, carry):
         gamma_prev, alpha_prev, beta_prev = carry
 
-        terms = [halves(dot(bc_ref[s], rb[s])) for s in range(2)]
-        parts = [terms[0][0], terms[1][0], terms[0][1], terms[1][1], zeros64b]
-        s1s[k] = dot(oht[...], jnp.concatenate(parts, axis=0)).astype(BF16).reshape(8, BLK, LOADS)
+        s1[k, grp] = jnp.concatenate([dot(bc_ref[s], rb[s]) for s in range(2)], axis=0).astype(BF16)
         for m in range(1, 8):
             s1_copy(k, m).start()
-        s1r[k, grp] = s1s[k, grp]
 
         gamma = jnp.zeros((8, LOADS), F32)
         delta = jnp.zeros((8, LOADS), F32)
@@ -284,12 +303,17 @@
                     fsend[k, f, s, i * 128 : i * 128 + 128, :] = fr.astype(BF16)
                     gamma = gamma + jnp.sum((r * r).reshape(16, 8, LOADS), axis=0)
                     delta = delta + jnp.sum((r * fr).reshape(16, 8, LOADS), axis=0)
-            if f != 3:
+            if f not in (0, 3):
                 face_copy(k, f).start()
             if place == 1:
+
+                @pl.when(k == 0)
+                def _():
+                    build_scatter()
+
                 for m in range(1, 8):
                     s1_copy(k, m).wait_recv()
-                total = add_slots(s1r, k, 8)
+                total = dot(scat[...], s1[k].reshape(2 * BLK, LOADS))
                 a1[k, zi] = total[:64]
                 b1[k, xi] = total[64:]
                 for m in range(1, 4):
@@ -309,27 +333,38 @@
         for m in range(1, 4):
             a2_copy(k, m).start()
             b2_copy(k, m).start()
-        face_copy(k, 3).start()
+        for m in range(1, 4):
+            a2_copy(k, m).wait_recv()
+            b2_copy(k, m).wait_recv()
+        s4[k, grp, :64, :] = add_slots(a2, k, 4)
+        s4[k, grp, 64:, :] = add_slots(b2, k, 4)
+        for m in range(1, 4):
+            y4_copy(k, m).start()
+        c4_copy(k, 0).start()
         for m in range(1, 4):
             d1_copy(k, m).wait_recv()
         d2[k, xi] = add_slots(d1, k, 4)
         for m in range(1, 4):
             d2_copy(k, m).start()
+        face_copy(k, 3).start()
+        face_copy(k, 0).start()
+
+        @pl.when(k == 0)
+        def _():
+            build_corners()
 
         @pl.when(k > 0)
         def _():
             follow(k - 1, beta_prev, alpha_prev)
 
         for m in range(1, 4):
-            a2_copy(k, m).wait_recv()
-            b2_copy(k, m).wait_recv()
             d2_copy(k, m).wait_recv()
-        s4[k, grp, :64, :] = add_slots(a2, k, 4)
-        s4[k, grp, 64:BLK, :] = add_slots(b2, k, 4)
-        s4[k, grp, BLK:, :] = add_slots(d2, k, 4)
-        for m in range(1, 4):
-            y4_copy(k, m).start()
-        c4_copy(k, 0).start()
+        d3[k, grp] = add_slots(d2, k, 4)
+        for m in range(1, 8):
+            d3_copy(k, m).start()
+        for m in range(1, 4):
+            y4_copy(k, m).wait_recv()
+            c4_copy(k, m).start()
 
         @pl.when(k == 0)
         def _():
@@ -350,10 +385,6 @@
                     )
                     frv[s, rows, :] = frv[s, rows, :] - received
 
-        for m in range(1, 4):
-            y4_copy(k, m).wait_recv()
-            c4_copy(k, m).start()
-
         @pl.when(k == 0)
         def _():
             sibling.wait_recv()
@@ -363,13 +394,13 @@
 
         for j in range(8):
             rows = slice(j * BLK, (j + 1) * BLK)
-            high, low = halves(s4[k, j, :BLK, :])
+            high, low = halves(s4[k, j])
             rb2[rows, :LOADS] = high
             rb2[rows, LOADS:] = low
         quad = jnp.zeros((8, LOADS), F32)
         for j in range(8):
             rows = slice(j * BLK, (j + 1) * BLK)
-            rhs = s4[k, j, :BLK, :]
+            rhs = s4[k, j]
             y = dot(cg[0, rows, :HALF], rb2[:HALF, :]) + dot(cg[1, rows, :HALF], rb2[HALF:, :])
             y = y[:, :LOADS] + y[:, LOADS:] + cg[0, rows, HALF:].astype(F32) * rhs
             quad = quad + jnp.sum((y * rhs).reshape(16, 8, LOADS), axis=0)
@@ -377,9 +408,9 @@
             yb[rows, :LOADS] = high
             yb[rows, LOADS:] = low
         quad = jnp.sum(quad, axis=0, keepdims=True)
-        tile = s4[k, 0, BLK:, :]
-        for j in range(1, 8):
-            tile = tile + s4[k, j, BLK:, :]
+        for m in range(1, 8):
+            d3_copy(k, m).wait_recv()
+        tile = add_slots(d3, k, 8)
         gamma = pick_row(tile, 0)
         delta = pick_row(tile, 1)
         picked = dot(oh[...], yb[...])
@@ -407,19 +438,6 @@
                     rv[k + 1, s, rows, :] = r
                     rb[s, rows, :] = r.astype(BF16)
 
-        for f in range(FACES):
-            face_copy(k, f).wait_send()
-            c4_copy(k, f).wait_send()
-        for m in range(1, 8):
-            s1_copy(k, m).wait_send()
-        for m in range(1, 4):
-            a1_copy(k, m).wait_send()
-            a2_copy(k, m).wait_send()
-            b1_copy(k, m).wait_send()
-            b2_copy(k, m).wait_send()
-            d1_copy(k, m).wait_send()
-            d2_copy(k, m).wait_send()
-            y4_copy(k, m).wait_send()
         return gamma, alpha, beta
 
     ones = jnp.ones((1, LOADS), F32)
@@ -430,11 +448,13 @@
     follow(ITERS - 1, beta, alpha)
     out_mult = pltpu.make_async_copy(xv, mult_hbm, load_sem.at[9])
     out_mult.start()
+    for k in range(ITERS):
+        sent(k)
     for f in range(FACES):
         gap_copy(f, 0).wait_send()
         gap_copy(f, 1).wait_send()
-        setup[f][0].wait_send()
-        setup[f][1].wait_send()
+    for copy in id_copies + b_copies:
+        copy.wait_send()
     core_copy.wait_send()
     sibling.wait_send()
     for copy in stage_y + stage_z + stage_x:
@@ -468,19 +488,20 @@
             pltpu.VMEM((2, NCG, WIDE), BF16),
             pltpu.VMEM((8, NCG), F32),
             pltpu.VMEM((160, NCG), BF16),
-            pltpu.VMEM((NCG, LOADS), BF16),
+            pltpu.VMEM((BLK, 2 * LOADS), BF16),
             pltpu.VMEM((2, FACES, NF, LOADS), BF16),
-            pltpu.VMEM((FACES, 2, NC, LOADS), jnp.int32),
+            pltpu.VMEM((8, 2, NC, LOADS), jnp.int32),
+            pltpu.VMEM((2, NC, LOADS), jnp.int32),
             pltpu.VMEM((FACES, 2, NC, NF), BF16),
-            pltpu.VMEM((ITERS, 8, BLK, LOADS), BF16),
-            pltpu.VMEM((ITERS, 8, BLK, LOADS), BF16),
+            pltpu.VMEM((ITERS, 8, 2 * NC, LOADS), BF16),
             pltpu.VMEM((ITERS, 4, 64, LOADS), F32),
             pltpu.VMEM((ITERS, 4, 64, LOADS), F32),
             pltpu.VMEM((ITERS, 4, 64, LOADS), F32),
             pltpu.VMEM((ITERS, 4, 64, LOADS), F32),
             pltpu.VMEM((ITERS, 4, 8, LOADS), F32),
             pltpu.VMEM((ITERS, 4, 8, LOADS), F32),
-            pltpu.VMEM((ITERS, 8, ROWS, LOADS), F32),
+            pltpu.VMEM((ITERS, 8, 8, LOADS), F32),
+            pltpu.VMEM((ITERS, 8, BLK, LOADS), F32),
             pltpu.VMEM((NCG, 2 * LOADS), BF16),
             pltpu.VMEM((NCG, 2 * LOADS), BF16),
             pltpu.VMEM((160, LOADS), F32),
@@ -495,7 +516,8 @@
             dma((ITERS, 8)),
         ]
         + [dma((ITERS, 4))] * 12
-        + [dma((ITERS, 8))] * 2,
+        + [dma((ITERS, 8))] * 4
+        + [dma((8,))] * 2,
         compiler_params=pltpu.CompilerParams(
             collective_id=0, has_side_effects=True, vmem_limit_bytes=60 * 1024 * 1024
         ),

time: 115 us -> 108 us (0.939); the launches traced: 114 us -> 108 us
  Pallas kernels: 107 us -> 102 us
    pallas_call x1, Pallas kernels: 107 us -> 102 us  [shards(): pl.pallas_call(kernel, out_shape=(field, field), in_specs=[pl.BlockSpec(m...]
where the time goes in v3:
time: 108 us
  Pallas kernels  102 us (94%)
  local copies, waits for them, and re-layouts  5.87 us (5%)
    pallas_call x1, Pallas kernels, shards(): pl.pallas_call(kernel, out_shape=(field, field), in_specs=[pl.BlockSpec(m...  102 us
    unnamed x4, local copies, waits for them, and re-layouts  4.52 us

profile of v3, /device:TPU:1, one launch (start us, length us, event | category | flops | bytes accessed | tf_op | source)
XLA Modules:
  0.0 108.2 jit_solution(13355814705333719910)
XLA Ops:
  0.6 1.4 %broadcast_in_dim.2.ids_ref = s32[2,16,128]{2,1,0:T(8,128)} broadcast(s32[2,16]{1,0:T(2,128)} %param.9), dimensions={0,1} | broadcast | bytes 16512 | tf_op jit(solution)/shard_map/broadcast_in_dim | solution.py:467
  2.0 101.7 %shard_map.77 = (f32[2,2048,128]{2,1,0:T(8,128)}, f32[2,2048,128]{2,1,0:T(8,128)}) custom-call(s32[2,4]{1,0:T(2,128)} %adj_ref.1, s32[2,16,128]{2,1,0:T(8,128)} %broadcast_in_dim.2.ids_ref, f32[8,1024]{1,0:T(8,128)} %cinv_ref.1, bf16[2,16,2048]{2,1,0:T(8,128)(2,1)} %bc_ref.1, bf16[2,2048,128]{2,1,0:T(8,128)(2,1)} %gap_hbm.1, bf16[2,2048,2048]{2,1,0:T(8,128)(2,1)} %flex_hbm.1), custom_call_target="tpu_custom_call" | custom-call | tf_op jit(solution)/shard_map/pallas_call | solution.py:472
  103.7 0.0 copy-start
  103.7 3.2 %copy.10 = f32[2,2048,128]{2,1,0:T(8,128)} copy(f32[2,2048,128]{2,1,0:T(8,128)} %get-tuple-element.4) | data formatting | bytes 4194304
  106.9 0.0 copy-done
  106.9 1.3 %copy.11 = f32[2,2048,128]{2,1,0:T(8,128)} copy(f32[2,2048,128]{2,1,0:T(8,128)S(1)} %copy-done) | data formatting | bytes 4194304
Async XLA Ops:
  103.7 3.2 %copy-start = (f32[2,2048,128]{2,1,0:T(8,128)S(1)}, f32[2,2048,128]{2,1,0:T(8,128)}, u32[]{:S(2)}) copy-start(f32[2,2048,128]{2,1,0:T(8,128)} %get-tuple-element.5) | copy-start | bytes 6291460

commit v4 on v3

--- a/solution.py
+++ b/solution.py
@@ -52,10 +52,10 @@
 
 
 def kernel(
-    adj_ref, ids_ref, cinv_ref, bc_ref, gap_hbm, flex_hbm,
+    adj_ref, raw_ref, cinv_ref, bc_ref, gap_hbm, flex_hbm,
     mult_hbm, res_hbm,
     fv, gapv, rv, pv, uv, xv, frv, rb, frecv, fsend,
-    cg, cex, oh, scat, bct, idg, idz, brecv,
+    cg, cex, oh, scat, bct, ids_ref, idg, idz, brecv,
     s1, a1, a2, b1, b2, d1, d2, d3, s4, rb2, yb, cv,
     load_sem, send0, recv0, sendg, recvg, sendf, recvf, send1, recv1,
     senda1, recva1, senda2, recva2, sendb1, recvb1, sendb2, recvb2,
@@ -73,6 +73,12 @@
             src_ref=src, dst_ref=dst, send_sem=send, recv_sem=recv,
             device_id=(flip(me, mask),), device_id_type=MESH,
         )
+
+    diagonal = lax.broadcasted_iota(jnp.int32, (NC, NC), 0) == lax.broadcasted_iota(jnp.int32, (NC, NC), 1)
+    for s in range(2):
+        row = jnp.broadcast_to(raw_ref[s : s + 1, :].astype(F32), (NC, NC))
+        column = jnp.sum(jnp.where(diagonal, row, 0.0), axis=1, keepdims=True)
+        ids_ref[s] = jnp.broadcast_to(column, (NC, LOADS))
 
     barrier = pltpu.get_barrier_semaphore()
     masks = [1, 2, 3, 4, 5, 6, 7, 8, 16, 24, 32, 64, 96]
@@ -139,7 +145,7 @@
         copy.start()
     idg[grp] = ids_ref[...]
 
-    lane = lax.broadcasted_iota(jnp.int32, (NC, LOADS), 1)
+    lane = lax.broadcasted_iota(jnp.int32, (NC, LOADS), 1).astype(F32)
 
     def one_hot(ids):
         return [jnp.where(ids == lane + b * LOADS, 1.0, 0.0).astype(F32) for b in range(NCG // LOADS)]
@@ -156,7 +162,7 @@
     def build_scatter():
         for copy in id_copies:
             copy.wait_recv()
-        mine = lane + grp * BLK
+        mine = lane + (grp * BLK).astype(F32)
         for q in range(2):
             tiles = [
                 jnp.where(idg[e, s] == mine, 1.0, 0.0).astype(F32)
@@ -464,7 +470,6 @@
 
 
 def shards(gap_loads, flexibility, corner_coupling, corner_ids, coarse_inverse, adjacency):
-    ids = jnp.broadcast_to(corner_ids[:, :, None], corner_ids.shape + (LOADS,))
     field = jax.ShapeDtypeStruct((2, NI, LOADS), F32)
     vmem = pl.BlockSpec(memory_space=pltpu.VMEM)
     hbm = pl.BlockSpec(memory_space=pl.ANY)
@@ -490,8 +495,9 @@
             pltpu.VMEM((160, NCG), BF16),
             pltpu.VMEM((BLK, 2 * LOADS), BF16),
             pltpu.VMEM((2, FACES, NF, LOADS), BF16),
-            pltpu.VMEM((8, 2, NC, LOADS), jnp.int32),
-            pltpu.VMEM((2, NC, LOADS), jnp.int32),
+            pltpu.VMEM((2, NC, LOADS), F32),
+            pltpu.VMEM((8, 2, NC, LOADS), F32),
+            pltpu.VMEM((2, NC, LOADS), F32),
             pltpu.VMEM((FACES, 2, NC, NF), BF16),
             pltpu.VMEM((ITERS, 8, 2 * NC, LOADS), BF16),
             pltpu.VMEM((ITERS, 4, 64, LOADS), F32),
@@ -521,7 +527,7 @@
         compiler_params=pltpu.CompilerParams(
             collective_id=0, has_side_effects=True, vmem_limit_bytes=60 * 1024 * 1024
         ),
-    )(adjacency, ids, coarse_inverse, corner_coupling, gap_loads, flexibility)
+    )(adjacency, corner_ids, coarse_inverse, corner_coupling, gap_loads, flexibility)
 
 
 def solution(mesh):

time: 108 us -> 108 us (level)
  local copies, waits for them, and re-layouts: 5.87 us -> 4.52 us
    broadcast_in_dim x1 -> x0, local copies, waits for them, and re-layouts: 1.35 us -> none  [shards(): ids = jnp.broadcast_to(corner_ids[:, :, None], corner_ids.shape + (LOADS,))]
where the time goes in v4:
time: 108 us
  Pallas kernels  102 us (94%)
  local copies, waits for them, and re-layouts  4.52 us (4%)
    pallas_call x1, Pallas kernels, shards(): pl.pallas_call(kernel, out_shape=(field, field), in_specs=[pl.BlockSpec(m...  102 us
    unnamed x4, local copies, waits for them, and re-layouts  4.52 us

profile of v4, /device:TPU:1, one launch (start us, length us, event | category | flops | bytes accessed | tf_op | source)
XLA Modules:
  0.0 107.5 jit_solution(9822964366807162754)
XLA Ops:
  0.6 102.4 %shard_map.77 = (f32[2,2048,128]{2,1,0:T(8,128)}, f32[2,2048,128]{2,1,0:T(8,128)}) custom-call(s32[2,4]{1,0:T(2,128)} %adj_ref.1, s32[2,16]{1,0:T(2,128)} %raw_ref.1, f32[8,1024]{1,0:T(8,128)} %cinv_ref.1, bf16[2,16,2048]{2,1,0:T(8,128)(2,1)} %bc_ref.1, bf16[2,2048,128]{2,1,0:T(8,128)(2,1)} %gap_hbm.1, bf16[2,2048,2048]{2,1,0:T(8,128)(2,1)} %flex_hbm.1), custom_call_target="tpu_custom_call" | custom-call | tf_op jit(solution)/shard_map/pallas_call | solution.py:477
  103.0 0.0 copy-start
  103.0 3.2 %copy.10 = f32[2,2048,128]{2,1,0:T(8,128)} copy(f32[2,2048,128]{2,1,0:T(8,128)} %get-tuple-element.4) | data formatting | bytes 4194304
  106.2 0.0 copy-done
  106.2 1.3 %copy.11 = f32[2,2048,128]{2,1,0:T(8,128)} copy(f32[2,2048,128]{2,1,0:T(8,128)S(1)} %copy-done) | data formatting | bytes 4194304
Async XLA Ops:
  103.0 3.2 %copy-start = (f32[2,2048,128]{2,1,0:T(8,128)S(1)}, f32[2,2048,128]{2,1,0:T(8,128)}, u32[]{:S(2)}) copy-start(f32[2,2048,128]{2,1,0:T(8,128)} %get-tuple-element.5) | copy-start | bytes 6291460
